TPU v7x, 256 devices: a whole 4x4x8 slice. The times are simulated.
256 devices in a mesh: dp: 4 (over y), expert: 8 (over z), etp: 8 (over x, core).
Axes of the slice: x: 4, y: 4, z: 8, core: 2. Of those that a mesh axis runs over, the one named last changes fastest.
Arguments:
- tokens: bfloat16 [4096, 3072], P(('dp', 'expert')), may hold values from -6 to 6
- grad_out: bfloat16 [4096, 3072], P(('dp', 'expert')), may hold values from -6 to 6
- gate_prob: float32 [4096, 2], P(('dp', 'expert')), may hold values from 0.1 to 1
- expert_ids: int32 [4096, 2], P(('dp', 'expert')), may hold values from 0 to 7, all different within a row; in each aligned block of 128 rows (0 to 127, 128 to 255, ...) at most 36 rows name the same one
- w_gate: bfloat16 [8, 3072, 8192], P('expert', None, ('dp', 'etp')), may hold values from -0.109375 to 0.109375
- w_up: bfloat16 [8, 3072, 8192], P('expert', None, ('dp', 'etp')), may hold values from -0.109375 to 0.109375
- w_down: bfloat16 [8, 8192, 3072], P('expert', ('dp', 'etp')), may hold values from -0.0625 to 0.0625
Outputs:
- grad_tokens: bfloat16 [4096, 3072], P(('dp', 'expert'), 'etp')
- grad_w_gate: bfloat16 [8, 3072, 8192], P('expert', None, ('dp', 'etp'))
- grad_w_up: bfloat16 [8, 3072, 8192], P('expert', None, ('dp', 'etp'))
- grad_w_down: bfloat16 [8, 8192, 3072], P('expert', ('dp', 'etp'))
Inputs may be any that keep to these rules, and one draw needn't show every extreme that they name: `expert_ids`: each row names two different experts. Within each aligned block of 128 rows no expert is named by more than 36 rows, a bound that some block reaches.
All inputs are finite; a program needn't handle non-finite values.
Results may differ from a plain program's by a relative error of at most 0.02.
Values may be sent and summed in bfloat16 or wider, within the bound.
No kernel may reach another device: no remote copies, remote signals or barrier semaphores. Data moves between devices by JAX's collectives and lax.ppermute only.
A program may use at most 128 MiB of HBM per device.

v0:
```python
import jax
import jax.numpy as jnp
from jax import lax
from jax.experimental import pallas as pl
from jax.experimental.pallas import tpu as pltpu
from jax.sharding import Mesh, PartitionSpec as P

BF = jnp.bfloat16
F32 = jnp.float32


def turn(a, axis, step):
    size = lax.axis_size(axis)
    return lax.ppermute(a, axis, [(i, (i + step) % size) for i in range(size)])


def swap(a):
    return lax.ppermute(a, "core", [(0, 1), (1, 0)])


def dot(a, b, dims):
    return lax.dot_general(a, b, (dims, ((), ())), preferred_element_type=F32)


def same(shape):
    return pl.BlockSpec(shape, lambda k, xi: (0,) * len(shape), pipeline_mode=pl.Buffered(1))


def call(body, grid, in_specs, out_specs, out_shape, args, flops, mib, scratch=()):
    return pl.pallas_call(
        body,
        grid_spec=pltpu.PrefetchScalarGridSpec(
            num_scalar_prefetch=1,
            grid=grid,
            in_specs=in_specs,
            out_specs=out_specs,
            scratch_shapes=scratch,
        ),
        out_shape=out_shape,
        compiler_params=pltpu.CompilerParams(
            dimension_semantics=("arbitrary",), vmem_limit_bytes=mib << 20
        ),
        cost_estimate=pl.CostEstimate(flops=int(flops), bytes_accessed=8 << 20, transcendentals=0),
    )(*args)


def pack(xi, own, theirs):
    width, hid = own[0].shape
    cols = width // 4
    up = pl.BlockSpec((cols, hid), lambda k, xi: ((xi[0] + k) % 4, 0))
    down = pl.BlockSpec((hid, cols), lambda k, xi: (0, (xi[0] + k) % 4))

    def body(xi, g1, u1, d1, g2, u2, d2, w, wd):
        for j, ref in enumerate((g1, u1, g2, u2)):
            w[:, j * hid : (j + 1) * hid] = ref[...]
        wd[:hid] = d1[...]
        wd[hid:] = d2[...]

    return call(
        body,
        (4,),
        [up, up, down] * 2,
        [
            pl.BlockSpec((cols, 4 * hid), lambda k, xi: (k, 0)),
            pl.BlockSpec((2 * hid, cols), lambda k, xi: (0, k)),
        ],
        [jax.ShapeDtypeStruct((width, 4 * hid), BF), jax.ShapeDtypeStruct((2 * hid, width), BF)],
        (xi, *own, *theirs),
        width * hid,
        14,
    )


def hidden_part(xi, pieces, w):
    rows, width = pieces[0].shape
    cols = width // 4
    every = rows * len(pieces)

    def body(xi, *refs):
        *xs, w, out = refs
        a = xs[0][...] if len(xs) == 1 else jnp.concatenate([x[...] for x in xs], axis=0)
        part = dot(a, w[...], ((1,), (0,)))
        first = pl.program_id(0) == 0

        @pl.when(first)
        def _():
            out[...] = part

        @pl.when(jnp.logical_not(first))
        def _():
            out[...] += part

    shape = jax.ShapeDtypeStruct((every, w.shape[1]), F32)
    return call(
        body,
        (4,),
        [pl.BlockSpec((rows, cols), lambda k, xi: (0, k))] * len(pieces)
        + [pl.BlockSpec((cols, w.shape[1]), lambda k, xi: (k, 0))],
        same(shape.shape),
        shape,
        (xi, *pieces, w),
        2 * every * width * w.shape[1],
        14,
    )


def down_part(xi, ys, places, wd, so_far=None):
    rows, cols = ys[0].shape
    n = len(ys)
    more = [] if so_far is None else [so_far]

    def body(xi, *refs):
        out = dot(refs[0][...], refs[n][...], ((1,), (1,)))
        for j in range(1, n):
            out += dot(refs[j][...], refs[n + j][...], ((1,), (1,)))
        if more:
            out += refs[2 * n][...]
        refs[-1][...] = out

    shape = jax.ShapeDtypeStruct((rows, wd.shape[0]), F32)
    return call(
        body,
        (1,),
        [same((rows, cols))] * n
        + [pl.BlockSpec((wd.shape[0], cols), lambda k, xi, j=j: (0, j)) for j in places]
        + [same(shape.shape)] * len(more),
        same(shape.shape),
        shape,
        (xi, *ys, *(wd,) * n, *more),
        2 * n * rows * cols * wd.shape[0],
        16,
    )


def token_part(xi, hu0, hu13, ga, x2a, x2b, y2a, y2b, w, wd):
    rows, side = x2a.shape
    width = 2 * side
    cols = width // 4
    hid = w.shape[1] // 4
    every = 4 * rows

    def body(xi, h0, h13, ga1, xa, xb, ya, yb, w, wd, act, g, pa, pb, h2):
        step = pl.program_id(0)

        @pl.when(step < 4)
        def _():
            part = dot(jnp.where(step < 2, xa[...], xb[...]), w[...], ((1,), (0,)))

            @pl.when(step == 0)
            def _():
                h2[...] = part

            @pl.when(step > 0)
            def _():
                h2[...] += part

        @pl.when(step == 3)
        def _():
            y2 = jnp.concatenate([ya[...], yb[...]], axis=0)
            for c in range(2):
                part = slice(c * hid, (c + 1) * hid)
                hs = slice(2 * c * hid, (2 * c + 1) * hid)
                us = slice((2 * c + 1) * hid, (2 * c + 2) * hid)
                ga2 = dot(y2, wd[part, :], ((1,), (1,)))
                for k, (ref, at) in enumerate(((h0, 0), (h13, 0), (h2, 0), (h13, rows))):
                    r = slice(k * rows, (k + 1) * rows)
                    hh = ref[at : at + rows, hs]
                    uu = ref[at : at + rows, us]
                    gg = ga1[r, part] + ga2[r]
                    s = jax.nn.sigmoid(hh)
                    silu = hh * s
                    act[r, part] = (silu * uu).astype(BF)
                    g[r, hs] = (gg * uu * (s * (1.0 + hh * (1.0 - s)))).astype(BF)
                    g[r, us] = (gg * silu).astype(BF)

        @pl.when(step > 3)
        def _():
            out = dot(g[...], w[...], ((1,), (1,))).astype(BF)
            pa[0] = out[:, : cols // 2]
            for k in range(4):
                pb[k] = out[k * rows : (k + 1) * rows, cols // 2 :]

    last = lambda k: jnp.maximum(k - 4, 0)
    shapes = [
        jax.ShapeDtypeStruct((every, 2 * hid), BF),
        jax.ShapeDtypeStruct((every, 4 * hid), BF),
        jax.ShapeDtypeStruct((4, every, cols // 2), BF),
        jax.ShapeDtypeStruct((4, rows, width // 2), BF),
    ]
    return call(
        body,
        (8,),
        [same(a.shape) for a in (hu0, hu13, ga)]
        + [
            pl.BlockSpec((rows, cols), lambda k, xi: (0, jnp.minimum(k, 1))),
            pl.BlockSpec((rows, cols), lambda k, xi: (0, jnp.clip(k - 2, 0, 1))),
            same(y2a.shape),
            same(y2b.shape),
            pl.BlockSpec((cols, 4 * hid), lambda k, xi: (k % 4, 0)),
            pl.BlockSpec((2 * hid, cols), lambda k, xi: (0, 2), pipeline_mode=pl.Buffered(1)),
        ],
        [
            same(shapes[0].shape),
            same(shapes[1].shape),
            pl.BlockSpec((1, every, cols // 2), lambda k, xi: (last(k), 0, 0)),
            pl.BlockSpec((4, rows, cols // 2), lambda k, xi: (0, 0, last(k))),
        ],
        shapes,
        (xi, hu0, hu13, ga, x2a, x2b, y2a, y2b, w, wd),
        2 * every * width * 4 * hid,
        24,
        [pltpu.VMEM((rows, 4 * hid), F32)],
    )


def weight_part(xi, xs, ys, act, g, which):
    xr, x1, x2a, x2b, x3 = xs
    rows, width = xr.shape
    cols = width // 4
    every = 4 * rows
    hid = act.shape[1] // 2
    x_spec = pl.BlockSpec((rows, cols), lambda k, xi: (0, k))
    a_spec = pl.BlockSpec((rows, cols), lambda k, xi: (0, jnp.minimum(k, 1)))
    b_spec = pl.BlockSpec((rows, cols), lambda k, xi: (0, jnp.maximum(k - 2, 0)))

    def body(xi, xrr, x1r, xar, xbr, x3r, y0r, y1r, yar, ybr, y3r, actr, gr, out, ybuf):
        k = pl.program_id(0)
        for j, y in ((0, y0r), (1, y1r), (3, y3r)):

            @pl.when(k == j)
            def _():
                ybuf[...] = y[...]

        @pl.when(k == 2)
        def _():
            ybuf[: every // 2] = yar[...]
            ybuf[every // 2 :] = ybr[...]

        x2 = jnp.where(k < 2, xar[...], xbr[...])
        x = jnp.concatenate([xrr[...], x1r[...], x2, x3r[...]], axis=0)
        out[:, : 2 * hid] = dot(x, gr[...], ((0,), (0,))).astype(BF)
        d = dot(actr[...], ybuf[...], ((0,), (0,))).astype(BF)
        for j in range(cols // hid):
            out[j * hid : (j + 1) * hid, 2 * hid :] = d[:, j * hid : (j + 1) * hid]

    return call(
        body,
        (4,),
        [x_spec, x_spec, a_spec, b_spec, x_spec]
        + [same(y.shape) for y in ys]
        + [
            pl.BlockSpec((every, hid), lambda k, xi: (0, which), pipeline_mode=pl.Buffered(1)),
            pl.BlockSpec((every, 2 * hid), lambda k, xi: (0, which), pipeline_mode=pl.Buffered(1)),
        ],
        pl.BlockSpec((cols, 3 * hid), lambda k, xi: (k, 0)),
        jax.ShapeDtypeStruct((width, 3 * hid), BF),
        (xi, *xs, *ys, act, g),
        2 * 3 * every * width * hid,
        22,
        [pltpu.VMEM((every, cols), BF)],
    )


def weight_sum(xi, mine, rest):
    width = mine.shape[0]
    hid = mine.shape[1] // 3
    cols = width // 4

    def body(xi, a, b, og, ou, od):
        s = (a[...].astype(F32) + b[...].astype(F32)).astype(BF)
        og[...] = s[:, :hid]
        ou[...] = s[:, hid : 2 * hid]
        for j in range(cols // hid):
            c = slice(j * hid, (j + 1) * hid)
            od[:, c] = s[c, 2 * hid :]

    up = pl.BlockSpec((cols, hid), lambda k, xi: ((xi[0] + k) % 4, 0))
    down = pl.BlockSpec((hid, cols), lambda k, xi: (0, (xi[0] + k) % 4))
    part = pl.BlockSpec((cols, 3 * hid), lambda k, xi: (k, 0))
    return call(
        body,
        (4,),
        [part, part],
        [up, up, down],
        [
            jax.ShapeDtypeStruct((width, hid), BF),
            jax.ShapeDtypeStruct((width, hid), BF),
            jax.ShapeDtypeStruct((hid, width), BF),
        ],
        (xi, mine, rest),
        width * hid,
        14,
    )


def add(*parts):
    out = parts[0].astype(F32)
    for p in parts[1:]:
        out = out + p.astype(F32)
    return out.astype(BF)


def tie(values, *late):
    out = lax.optimization_barrier((tuple(values), tuple(late)))
    return out[0]


def shards(tokens, grad_out, gate_prob, expert_ids, w_gate, w_up, w_down):
    rows, width = tokens.shape
    experts = lax.axis_size("expert")
    nx = lax.axis_size("x")
    nd = lax.axis_size("dp")
    capacity = rows * 9 // (4 * experts)
    half = capacity // 2
    cols = width // nx
    xi = lax.axis_index("x")
    core = lax.axis_index("core")
    at = xi.astype(jnp.int32).reshape(1)
    own = (w_gate[0], w_up[0], w_down[0])
    theirs = [swap(w) for w in own]

    ids = expert_ids.T
    lanes = jnp.arange(experts, dtype=jnp.int32)[:, None]
    named = [ids[k][None, :] == lanes for k in range(2)]
    member = named[0] | named[1]
    before = (
        jnp.arange(rows, dtype=jnp.int32)[:, None] < jnp.arange(rows, dtype=jnp.int32)[None, :]
    ).astype(BF)
    slot = dot(member.astype(BF), before, ((1,), (0,))).astype(jnp.int32)
    slot = jnp.where(member, slot, -1)
    gates = gate_prob.T
    gate = jnp.where(named[0], gates[0][None, :], 0.0) + jnp.where(
        named[1], gates[1][None, :], 0.0
    )
    mine = core * half + jnp.arange(half, dtype=jnp.int32)
    hit = slot[:, None, :] == mine[None, :, None]
    slot_gate = jnp.sum(jnp.where(hit, gate[:, None, :], 0.0), axis=2).reshape(-1, 1)
    pick = hit.astype(BF).reshape(experts * half, rows)
    every = jnp.arange(capacity, dtype=jnp.int32)
    pick_all = (
        (slot[:, None, :] == every[None, :, None])
        .astype(BF)
        .reshape(experts, 2, half, rows)
        .swapaxes(0, 1)
        .reshape(2 * experts * half, rows)
    )

    tok_cols = lax.dynamic_slice_in_dim(tokens, xi * cols, cols, 1)
    out_cols = lax.dynamic_slice_in_dim(grad_out, xi * cols, cols, 1)
    send_x = dot(pick, tok_cols, ((1,), (0,))).astype(BF).reshape(experts, half, cols)
    send_y = (dot(pick, out_cols, ((1,), (0,))) * slot_gate).astype(BF)
    send_y = send_y.reshape(experts, half, cols)
    sent = jnp.concatenate([send_x, send_y], axis=1)
    got = lax.all_to_all(sent, "expert", split_axis=0, concat_axis=0, tiled=True)
    w, wd = pack(at, own, theirs)
    (got,) = tie((got,), w, wd)
    x0 = got[:, :half].reshape(experts * half, cols)
    y0 = got[:, half:].reshape(experts * half, cols)
    xs = [x0, turn(x0, "x", -1), turn(x0, "x", 2), turn(x0, "x", 1)]
    ys = [y0, turn(y0, "dp", -1), turn(y0, "dp", 2), turn(y0, "dp", 1)]
    xr = jnp.concatenate(xs, axis=1)
    yc = jnp.concatenate(ys, axis=0)
    x1, x3 = turn(xr, "dp", -1), turn(xr, "dp", 1)
    y1, y3 = turn(yc, "x", -1), turn(yc, "x", 1)
    hu0 = hidden_part(at, (xr,), w)
    ga0 = down_part(at, (yc,), (0,), wd)
    x1, x3, y1, y3 = tie((x1, x3, y1, y3), hu0, ga0)
    hx, hy = width // 2, yc.shape[0] // 2
    x2a, x2b = turn(x1[:, :hx], "dp", -1), turn(x3[:, hx:], "dp", 1)
    y2a, y2b = turn(y1[:hy], "x", -1), turn(y3[hy:], "x", 1)
    hu13 = hidden_part(at, (x1, x3), w)
    ga = down_part(at, (y1, y3), (1, 3), wd, ga0)
    x2a, x2b, y2a, y2b = tie((x2a, x2b, y2a, y2b), hu13, ga)
    act, g, pa, pb = token_part(at, hu0, hu13, ga, x2a, x2b, y2a, y2b, w, wd)

    ra, rb = pa.shape[1] // 2, pb.shape[2] // 2
    a_up, a_dn = turn(pa[2, :ra], "x", 1), turn(pa[2, ra:], "x", -1)
    b_up, b_dn = turn(pb[2, :, :rb], "dp", 1), turn(pb[2, :, rb:], "dp", -1)
    x_all, y_all = (xr, x1, x2a, x2b, x3), (yc, y1, y2a, y2b, y3)
    part = weight_part(at, x_all, y_all, act, g, 1)
    a_up, a_dn, b_up, b_dn, part = tie((a_up, a_dn, b_up, b_dn, part))
    part = swap(part)
    a1 = jnp.concatenate([add(pa[1, :ra], a_up), pa[1, ra:]], axis=0)
    a3 = jnp.concatenate([pa[3, :ra], add(pa[3, ra:], a_dn)], axis=0)
    b1 = jnp.concatenate([add(pb[1, :, :rb], b_up), pb[1, :, rb:]], axis=1)
    b3 = jnp.concatenate([pb[3, :, :rb], add(pb[3, :, rb:], b_dn)], axis=1)
    a1, a3 = turn(a1, "x", 1), turn(a3, "x", -1)
    b1, b3 = turn(b1, "dp", 1), turn(b3, "dp", -1)
    mine = weight_part(at, x_all, y_all, act, g, 0)
    a1, a3, b1, b3 = tie((a1, a3, b1, b3), mine)
    sa = add(pa[0], a1, a3).reshape(nd, -1, cols // 2)
    sb = add(pb[0], b1, b3)
    qa = [turn(sa[k], "dp", k) for k in range(1, nd)]
    qb = [turn(sb[:, k * cols // 2 : (k + 1) * cols // 2], "x", k) for k in range(1, nx)]
    ga_x = add(sa[0], *qa)
    gb_x = add(sb[:, : cols // 2], *qb)

    back = jnp.stack(
        [g.reshape(experts, half, cols // 2) for g in (ga_x, gb_x)], axis=1
    ).reshape(experts * 2, half, cols // 2)
    back = lax.all_to_all(back, ("expert", "core"), split_axis=0, concat_axis=0, tiled=True)
    gw_gate, gw_up, gw_down = weight_sum(at, mine, part)
    (back,) = tie((back,), gw_gate)
    back = back.reshape(experts, 2, half, cols // 2).transpose(1, 0, 2, 3)
    back = back.reshape(2 * experts * half, cols // 2)
    grad_tokens = dot(pick_all, back, ((0,), (0,))).astype(BF)
    return grad_tokens, gw_gate[None], gw_up[None], gw_down[None]


def solution(mesh):
    sizes = mesh.devices.shape
    fine = Mesh(
        mesh.devices.reshape(sizes[0], sizes[1], sizes[2] // 2, 2), ("dp", "expert", "x", "core")
    )
    by_token = P(("dp", "expert"), None)
    up = P("expert", None, ("dp", "x", "core"))
    down = P("expert", ("dp", "x", "core"), None)
    return jax.shard_map(
        shards,
        mesh=fine,
        in_specs=(by_token, by_token, by_token, by_token, up, up, down),
        out_specs=(P(("dp", "expert"), ("x", "core")), up, up, down),
        check_vma=False,
    )
```

profile of v0, /device:TPU:1, one launch (start us, length us, event | category | flops | bytes accessed | tf_op | source)
XLA Modules:
  0.0 164.9 jit_solution(4950578622811700360)
XLA Ops:
  0.6 3.3 %collective-permute-start = (bf16[3072,256]{1,0:T(8,128)(2,1)}, bf16[3072,256]{1,0:T(8,128)(2,1)S(1)}, u32[]{:S(2)}, u32[]{:S(2)}) collective-permute-start(bf16[3072,256]{1,0:T(8,128)(2,1)} %bitcast.64), channel_id=1, source_target_pairs={{0,1},{1,0},{2,3},{3,2},{4,5},{5,4},{6,7},{7,6},{8,9},{9,8},{10,11... | collective-permute-start | bytes 4718600 | tf_op jit(solution)/shard_map/ppermute | solution.py:18
  6.9 1.1 convolution_convert_fusion
  9.0 6.5 %all-to-all-start = ((bf16[8,36,768]{2,1,0:T(8,128)(2,1)}), bf16[8,36,768]{2,1,0:T(8,128)(2,1)}, u32[]{:S(2)}, u32[]{:S(2)}) async-start(bf16[8,36,768]{2,1,0:T(8,128)(2,1)} %pad_maximum_fusion), calls=%async_computation | async-start | bytes 983040 | tf_op jit(solution)/shard_map/all_to_all | solution.py:354
  15.5 1.1 copy-done.9
  16.7 1.4 copy-done.6
  18.1 1.4 copy-done.7
  19.5 1.4 copy-done.8
  20.9 1.4 copy-done.10
  22.3 3.5 %shard_map.102 = (bf16[3072,1024]{1,0:T(8,128)(2,1)S(1)}, bf16[512,3072]{1,0:T(8,128)(2,1)S(1)}) custom-call(s32[1]{0:T(128)} %bitcast.3.xi, bf16[3072,256]{1,0:T(8,128)(2,1)S(1)} %bitcast.65, bf16[3072,256]{1,0:T(8,128)(2,1)S(1)} %bitcast.67, bf16[256,3072]{1,0:T(8,128)(2,1)S(1)} %bitcast.69, bf16[3072,256]{1,0:T(8,128)(2,1)S(1)} %copy-done.10, ...), custom_call_target="tpu_custom_call" | custom-call | flops 786432 | bytes 8388608 | tf_op jit(solution)/shard_map/pallas_call | solution.py:30
  25.8 2.7 %copy-done.2 = bf16[3072,1024]{1,0:T(8,128)(2,1)} copy-done((bf16[3072,1024]{1,0:T(8,128)(2,1)}, bf16[3072,1024]{1,0:T(8,128)(2,1)S(1)}, u32[]{:S(2)}) %copy-start.2) | copy-done | bytes 6291480
  28.5 4.4 %all-to-all-done = bf16[8,36,768]{2,1,0:T(8,128)(2,1)} async-done(((bf16[8,36,768]{2,1,0:T(8,128)(2,1)}), bf16[8,36,768]{2,1,0:T(8,128)(2,1)}, u32[]{:S(2)}, u32[]{:S(2)}) %all-to-all-start) | async-done | bytes 442400 | tf_op jit(solution)/shard_map/all_to_all | solution.py:354
  32.9 1.8 %fusion.23 = (bf16[8,18,768]{2,1,0:T(8,128)(2,1)}, bf16[8,18,768]{2,1,0:T(8,128)(2,1)S(1)}) fusion(bf16[8,36,768]{2,1,0:T(8,128)(2,1)} %all-to-all-done), kind=kLoop, calls=%fused_computation.69 | loop fusion | bytes 884736 | tf_op jit(solution)/shard_map/slice | solution.py:358
  34.7 1.7 %reshape.131 = bf16[144,768]{1,0:T(8,128)(2,1)} reshape(bf16[8,18,768]{2,1,0:T(8,128)(2,1)} %get-tuple-element.72) | data formatting | bytes 442368 | tf_op jit(solution)/shard_map/reshape | solution.py:358
  36.4 2.7 %collective-permute-start.8 = (bf16[144,768]{1,0:T(8,128)(2,1)}, bf16[144,768]{1,0:T(8,128)(2,1)}, u32[]{:S(2)}, u32[]{:S(2)}) collective-permute-start(bf16[144,768]{1,0:T(8,128)(2,1)} %reshape.131), channel_id=1, source_target_pairs={{0,192},{64,0},{128,64},{192,128},{1,193},{65,1},{129,65},{193,129... | collective-permute-start | bytes 663560 | tf_op jit(solution)/shard_map/ppermute | solution.py:14
  41.0 2.5 %collective-permute-start.3 = (bf16[144,768]{1,0:T(8,128)(2,1)}, bf16[144,768]{1,0:T(8,128)(2,1)S(1)}, u32[]{:S(2)}, u32[]{:S(2)}) collective-permute-start(bf16[144,768]{1,0:T(8,128)(2,1)} %reshape.130), channel_id=1, source_target_pairs={{0,6},{2,0},{4,2},{6,4},{1,7},{3,1},{5,3},{7,5},{8,14},{10,8},{12,... | collective-permute-start | bytes 663560 | tf_op jit(solution)/shard_map/ppermute | solution.py:14
  45.9 2.5 %collective-permute-done.8 = bf16[144,768]{1,0:T(8,128)(2,1)} collective-permute-done((bf16[144,768]{1,0:T(8,128)(2,1)}, bf16[144,768]{1,0:T(8,128)(2,1)}, u32[]{:S(2)}, u32[]{:S(2)}) %collective-permute-start.8) | collective-permute-done | bytes 221216 | tf_op jit(solution)/shard_map/ppermute | solution.py:14
  48.4 1.2 collective-permute-start.5
  51.5 1.5 collective-permute-done.10
  54.0 2.6 %collective-permute-start.11 = (bf16[576,768]{1,0:T(8,128)(2,1)S(1)}, bf16[576,768]{1,0:T(8,128)(2,1)S(1)}, u32[]{:S(2)}, u32[]{:S(2)}) collective-permute-start(bf16[576,768]{1,0:T(8,128)(2,1)S(1)} %constant_dynamic-update-slice_fusion.4.refs_0_.y0r), channel_id=1, source_target_pairs={{0,6},{2,0},{4,2},{6,4},{1,7},{3,1},{5,3},{7,5},{8,14},{10,8},{12,... | collective-permute-start | bytes 2654216 | tf_op jit(solution)/shard_map/ppermute | solution.py:14
  56.7 2.4 %collective-permute-start.6 = (bf16[144,3072]{1,0:T(8,128)(2,1)S(1)}, bf16[144,3072]{1,0:T(8,128)(2,1)S(1)}, u32[]{:S(2)}, u32[]{:S(2)}) collective-permute-start(bf16[144,3072]{1,0:T(8,128)(2,1)S(1)} %constant_dynamic-update-slice_fusion.refs_0_.xrr), channel_id=1, source_target_pairs={{0,192},{64,0},{128,64},{192,128},{1,193},{65,1},{129,65},{193,129... | collective-permute-start | bytes 2654216 | tf_op jit(solution)/shard_map/ppermute | solution.py:14
  59.8 2.0 %shard_map.103.h0 = f32[144,1024]{1,0:T(8,128)S(1)} custom-call(s32[1]{0:T(128)} %bitcast.3.xi, bf16[144,3072]{1,0:T(8,128)(2,1)S(1)} %constant_dynamic-update-slice_fusion.refs_0_.xrr, bf16[3072,1024]{1,0:T(8,128)(2,1)S(1)} %copy-done.3), custom_call_target="tpu_custom_call" | custom-call | flops 905969664 | bytes 8388608 | tf_op jit(solution)/shard_map/pallas_call | solution.py:30
  61.7 13.4 %collective-permute-done.11.refs_0_.y1r = bf16[576,768]{1,0:T(8,128)(2,1)S(1)} collective-permute-done((bf16[576,768]{1,0:T(8,128)(2,1)S(1)}, bf16[576,768]{1,0:T(8,128)(2,1)S(1)}, u32[]{:S(2)}, u32[]{:S(2)}) %collective-permute-start.11) | collective-permute-done | bytes 884768 | tf_op jit(solution)/shard_map/ppermute | solution.py:14
  75.1 3.1 %collective-permute-done.12.refs_1_.y3r = bf16[576,768]{1,0:T(8,128)(2,1)S(1)} collective-permute-done((bf16[576,768]{1,0:T(8,128)(2,1)S(1)}, bf16[576,768]{1,0:T(8,128)(2,1)S(1)}, u32[]{:S(2)}, u32[]{:S(2)}) %collective-permute-start.12) | collective-permute-done | bytes 884768 | tf_op jit(solution)/shard_map/ppermute | solution.py:14
  79.5 1.3 collective-permute-start.14
  80.8 1.1 collective-permute-start.15
  82.5 1.1 shard_map.106.ga1
  83.6 3.1 %shard_map.105.h13 = f32[288,1024]{1,0:T(8,128)S(1)} custom-call(s32[1]{0:T(128)} %bitcast.3.xi, bf16[144,3072]{1,0:T(8,128)(2,1)S(1)} %collective-permute-done.6.refs_0_.x1r, bf16[144,3072]{1,0:T(8,128)(2,1)S(1)} %collective-permute-done.7.refs_1_.x3r, bf16[3072,1024]{1,0:T(8,128)(2,1)S(1)} %copy-done.3), custom_call_target="tpu_custom_call" | custom-call | flops 1811939328 | bytes 8388608 | tf_op jit(solution)/shard_map/pallas_call | solution.py:30
  87.4 1.6 collective-permute-done.14.xb.xbr
  89.0 1.6 collective-permute-done.16.yb.ybr
  90.7 8.2 %shard_map.107 = (bf16[576,512]{1,0:T(8,128)(2,1)S(1)}, bf16[576,1024]{1,0:T(8,128)(2,1)S(1)}, bf16[4,576,384]{2,1,0:T(8,128)(2,1)S(1)}, bf16[4,144,1536]{2,1,0:T(8,128)(2,1)S(1)}) custom-call(s32[1]{0:T(128)} %bitcast.3.xi, f32[144,1024]{1,0:T(8,128)S(1)} %shard_map.103.h0, f32[288,1024]{1,0:T(8,128)S(1)} %shard_map.105.h13, ...), custom_call_target="tpu_custom_call" | custom-call | flops 3623878656 | bytes 8388608 | tf_op jit(solution)/shard_map/pallas_call | solution.py:30
  99.1 2.7 %collective-permute-start.18 = (bf16[288,384]{1,0:T(8,128)(2,1)S(1)}, bf16[288,384]{1,0:T(8,128)(2,1)S(1)}, u32[]{:S(2)}, u32[]{:S(2)}) collective-permute-start(bf16[288,384]{1,0:T(8,128)(2,1)S(1)} %get-tuple-element.68), channel_id=1, source_target_pairs={{0,6},{2,0},{4,2},{6,4},{1,7},{3,1},{5,3},{7,5},{8,14},{10,8},{12,... | collective-permute-start | bytes 663560 | tf_op jit(solution)/shard_map/ppermute | solution.py:14
  101.9 2.7 %collective-permute-start.20 = (bf16[144,768]{1,0:T(8,128)(2,1)S(1)}, bf16[144,768]{1,0:T(8,128)(2,1)S(1)}, u32[]{:S(2)}, u32[]{:S(2)}) collective-permute-start(bf16[144,768]{1,0:T(8,128)(2,1)S(1)} %get-tuple-element.62), channel_id=1, source_target_pairs={{0,192},{64,0},{128,64},{192,128},{1,193},{65,1},{129,65},{193,129... | collective-permute-start | bytes 663560 | tf_op jit(solution)/shard_map/ppermute | solution.py:14
  104.5 6.4 %shard_map.108 = bf16[3072,768]{1,0:T(8,128)(2,1)} custom-call(s32[1]{0:T(128)} %bitcast.3.xi, bf16[144,3072]{1,0:T(8,128)(2,1)S(1)} %constant_dynamic-update-slice_fusion.refs_0_.xrr, bf16[144,3072]{1,0:T(8,128)(2,1)S(1)} %collective-permute-done.6.refs_0_.x1r, bf16[144,1536]{1,0:T(8,128)(2,1)S(1)} %collective-permute-done.13.xa.xar, ...), custom_call_target="tpu_custom_call" | custom-call | flops 2717908992 | bytes 8388608 | tf_op jit(solution)/shard_map/pallas_call | solution.py:30
  110.9 6.7 %collective-permute-start.31 = (bf16[3072,768]{1,0:T(8,128)(2,1)}, bf16[3072,768]{1,0:T(8,128)(2,1)}, u32[]{:S(2)}, u32[]{:S(2)}) collective-permute-start(bf16[3072,768]{1,0:T(8,128)(2,1)} %shard_map.108), channel_id=1, source_target_pairs={{0,1},{1,0},{2,3},{3,2},{4,5},{5,4},{6,7},{7,6},{8,9},{9,8},{10,11... | collective-permute-start | bytes 14155784 | tf_op jit(solution)/shard_map/ppermute | solution.py:18
  118.3 1.4 collective-permute-start.23
  120.0 1.5 collective-permute-start.21
  121.5 5.4 %shard_map.109.a = bf16[3072,768]{1,0:T(8,128)(2,1)S(1)} custom-call(s32[1]{0:T(128)} %bitcast.3.xi, bf16[144,3072]{1,0:T(8,128)(2,1)S(1)} %constant_dynamic-update-slice_fusion.refs_0_.xrr, bf16[144,3072]{1,0:T(8,128)(2,1)S(1)} %collective-permute-done.6.refs_0_.x1r, bf16[144,1536]{1,0:T(8,128)(2,1)S(1)} %collective-permute-done.13.xa.xar, ...), custom_call_target="tpu_custom_call" | custom-call | flops 2717908992 | bytes 8388608 | tf_op jit(solution)/shard_map/pallas_call | solution.py:30
  126.9 2.2 %copy-done.4 = bf16[3072,768]{1,0:T(8,128)(2,1)} copy-done((bf16[3072,768]{1,0:T(8,128)(2,1)}, bf16[3072,768]{1,0:T(8,128)(2,1)S(1)}, u32[]{:S(2)}) %copy-start.4) | copy-done | bytes 4718616
  129.7 1.6 collective-permute-done.23
  131.3 1.1 collective-permute-done.21
  133.1 2.4 %collective-permute-start.26 = (bf16[144,384]{1,0:T(8,128)(2,1)S(1)}, bf16[144,384]{1,0:T(8,128)(2,1)S(1)}, u32[]{:S(2)}, u32[]{:S(2)}) collective-permute-start(bf16[144,384]{1,0:T(8,128)(2,1)S(1)} %get-tuple-element.76), channel_id=1, source_target_pairs={{0,128},{64,192},{128,0},{192,64},{1,129},{65,193},{129,1},{193,65... | collective-permute-start | bytes 331784 | tf_op jit(solution)/shard_map/ppermute | solution.py:14
  135.9 1.7 %collective-permute-done.25 = bf16[144,384]{1,0:T(8,128)(2,1)S(1)} collective-permute-done((bf16[144,384]{1,0:T(8,128)(2,1)S(1)}, bf16[144,384]{1,0:T(8,128)(2,1)S(1)}, u32[]{:S(2)}, u32[]{:S(2)}) %collective-permute-start.25) | collective-permute-done | bytes 110624 | tf_op jit(solution)/shard_map/ppermute | solution.py:14
  138.1 1.2 collective-permute-done.26
  141.0 1.8 %collective-permute-done.29 = bf16[144,384]{1,0:T(8,128)(2,1)S(1)} collective-permute-done((bf16[144,384]{1,0:T(8,128)(2,1)S(1)}, bf16[144,384]{1,0:T(8,128)(2,1)S(1)}, u32[]{:S(2)}, u32[]{:S(2)}) %collective-permute-start.29) | collective-permute-done | bytes 110624 | tf_op jit(solution)/shard_map/ppermute | solution.py:14
  144.1 7.1 %all-to-all-start.1 = ((bf16[16,18,384]{2,1,0:T(8,128)(2,1)}), bf16[16,18,384]{2,1,0:T(8,128)(2,1)S(1)}, u32[]{:S(2)}, u32[]{:S(2)}) async-start(bf16[16,18,384]{2,1,0:T(8,128)(2,1)} %bitcast.24), calls=%async_computation.1 | async-start | bytes 589824 | tf_op jit(solution)/shard_map/all_to_all | solution.py:401
  151.2 2.3 %copy-done.5 = bf16[3072,768]{1,0:T(8,128)(2,1)S(1)} copy-done((bf16[3072,768]{1,0:T(8,128)(2,1)S(1)}, bf16[3072,768]{1,0:T(8,128)(2,1)}, u32[]{:S(2)}) %copy-start.5) | copy-done | bytes 4718616
  153.6 5.3 %shard_map.110 = (bf16[3072,256]{1,0:T(8,128)(2,1)}, bf16[3072,256]{1,0:T(8,128)(2,1)}, bf16[256,3072]{1,0:T(8,128)(2,1)}) custom-call(s32[1]{0:T(128)} %bitcast.3.xi, bf16[3072,768]{1,0:T(8,128)(2,1)S(1)} %copy-done.5, bf16[3072,768]{1,0:T(8,128)(2,1)} %collective-permute-done.31.b), custom_call_target="tpu_custom_call" | custom-call | flops 786432 | bytes 8388608 | tf_op jit(solution)/shard_map/pallas_call | solution.py:30
  158.9 4.8 %all-to-all-done.1 = bf16[16,18,384]{2,1,0:T(8,128)(2,1)S(1)} async-done(((bf16[16,18,384]{2,1,0:T(8,128)(2,1)}), bf16[16,18,384]{2,1,0:T(8,128)(2,1)S(1)}, u32[]{:S(2)}, u32[]{:S(2)}) %all-to-all-start.1) | async-done | bytes 221216 | tf_op jit(solution)/shard_map/all_to_all | solution.py:401
  (104 shorter events, 21.8 us)
Async XLA Ops:
  0.6 6.0 %copy-start = (bf16[128,3072]{1,0:T(8,128)(2,1)S(1)}, bf16[128,3072]{1,0:T(8,128)(2,1)}, u32[]{:S(2)}) copy-start(bf16[128,3072]{1,0:T(8,128)(2,1)} %param.8) | copy-start | bytes 2359300
  0.6 14.9 %collective-permute-start = (bf16[3072,256]{1,0:T(8,128)(2,1)}, bf16[3072,256]{1,0:T(8,128)(2,1)S(1)}, u32[]{:S(2)}, u32[]{:S(2)}) collective-permute-start(bf16[3072,256]{1,0:T(8,128)(2,1)} %bitcast.64), channel_id=1, source_target_pairs={{0,1},{1,0},{2,3},{3,2},{4,5},{5,4},{6,7},{7,6},{8,9},{9,8},{10,11... | collective-permute-start | bytes 4718600 | tf_op jit(solution)/shard_map/ppermute | solution.py:18
  4.0 12.7 %collective-permute-start.1 = (bf16[3072,256]{1,0:T(8,128)(2,1)}, bf16[3072,256]{1,0:T(8,128)(2,1)}, u32[]{:S(2)}, u32[]{:S(2)}) collective-permute-start(bf16[3072,256]{1,0:T(8,128)(2,1)} %bitcast.66), channel_id=1, source_target_pairs={{0,1},{1,0},{2,3},{3,2},{4,5},{5,4},{6,7},{7,6},{8,9},{9,8},{10,11... | collective-permute-start | bytes 4718600 | tf_op jit(solution)/shard_map/ppermute | solution.py:18
  4.1 12.6 %collective-permute-start.2 = (bf16[256,3072]{1,0:T(8,128)(2,1)}, bf16[256,3072]{1,0:T(8,128)(2,1)}, u32[]{:S(2)}, u32[]{:S(2)}) collective-permute-start(bf16[256,3072]{1,0:T(8,128)(2,1)} %bitcast.68), channel_id=1, source_target_pairs={{0,1},{1,0},{2,3},{3,2},{4,5},{5,4},{6,7},{7,6},{8,9},{9,8},{10,11... | collective-permute-start | bytes 4718600 | tf_op jit(solution)/shard_map/ppermute | solution.py:18
  9.0 23.9 %all-to-all-start = ((bf16[8,36,768]{2,1,0:T(8,128)(2,1)}), bf16[8,36,768]{2,1,0:T(8,128)(2,1)}, u32[]{:S(2)}, u32[]{:S(2)}) async-start(bf16[8,36,768]{2,1,0:T(8,128)(2,1)} %pad_maximum_fusion), calls=%async_computation | async-start | bytes 983040 | tf_op jit(solution)/shard_map/all_to_all | solution.py:354
  15.5 1.1 copy-start.9
  16.7 1.4 copy-start.6
  18.1 1.4 copy-start.7
  19.5 1.4 copy-start.8
  20.9 1.4 copy-start.10
  25.8 2.7 %copy-start.2 = (bf16[3072,1024]{1,0:T(8,128)(2,1)}, bf16[3072,1024]{1,0:T(8,128)(2,1)S(1)}, u32[]{:S(2)}) copy-start(bf16[3072,1024]{1,0:T(8,128)(2,1)S(1)} %get-tuple-element.32.refs_1_.refs_2_.w) | copy-start | bytes 18874372
  36.4 12.0 %collective-permute-start.8 = (bf16[144,768]{1,0:T(8,128)(2,1)}, bf16[144,768]{1,0:T(8,128)(2,1)}, u32[]{:S(2)}, u32[]{:S(2)}) collective-permute-start(bf16[144,768]{1,0:T(8,128)(2,1)} %reshape.131), channel_id=1, source_target_pairs={{0,192},{64,0},{128,64},{192,128},{1,193},{65,1},{129,65},{193,129... | collective-permute-start | bytes 663560 | tf_op jit(solution)/shard_map/ppermute | solution.py:14
  39.2 11.4 %collective-permute-start.9 = (bf16[144,768]{1,0:T(8,128)(2,1)}, bf16[144,768]{1,0:T(8,128)(2,1)}, u32[]{:S(2)}, u32[]{:S(2)}) collective-permute-start(bf16[144,768]{1,0:T(8,128)(2,1)} %reshape.131), channel_id=1, source_target_pairs={{0,128},{64,192},{128,0},{192,64},{1,129},{65,193},{129,1},{193,65... | collective-permute-start | bytes 663560 | tf_op jit(solution)/shard_map/ppermute | solution.py:14
  39.5 13.6 %collective-permute-start.10 = (bf16[144,768]{1,0:T(8,128)(2,1)}, bf16[144,768]{1,0:T(8,128)(2,1)}, u32[]{:S(2)}, u32[]{:S(2)}) collective-permute-start(bf16[144,768]{1,0:T(8,128)(2,1)} %reshape.131), channel_id=1, source_target_pairs={{0,64},{64,128},{128,192},{192,0},{1,65},{65,129},{129,193},{193,1... | collective-permute-start | bytes 663560 | tf_op jit(solution)/shard_map/ppermute | solution.py:14
  41.0 15.6 %collective-permute-start.3 = (bf16[144,768]{1,0:T(8,128)(2,1)}, bf16[144,768]{1,0:T(8,128)(2,1)S(1)}, u32[]{:S(2)}, u32[]{:S(2)}) collective-permute-start(bf16[144,768]{1,0:T(8,128)(2,1)} %reshape.130), channel_id=1, source_target_pairs={{0,6},{2,0},{4,2},{6,4},{1,7},{3,1},{5,3},{7,5},{8,14},{10,8},{12,... | collective-permute-start | bytes 663560 | tf_op jit(solution)/shard_map/ppermute | solution.py:14
  43.4 13.2 %collective-permute-start.4 = (bf16[144,768]{1,0:T(8,128)(2,1)}, bf16[144,768]{1,0:T(8,128)(2,1)S(1)}, u32[]{:S(2)}, u32[]{:S(2)}) collective-permute-start(bf16[144,768]{1,0:T(8,128)(2,1)} %reshape.130), channel_id=1, source_target_pairs={{0,4},{2,6},{4,0},{6,2},{1,5},{3,7},{5,1},{7,3},{8,12},{10,14},{12... | collective-permute-start | bytes 663560 | tf_op jit(solution)/shard_map/ppermute | solution.py:14
  48.4 8.3 %collective-permute-start.5 = (bf16[144,768]{1,0:T(8,128)(2,1)}, bf16[144,768]{1,0:T(8,128)(2,1)S(1)}, u32[]{:S(2)}, u32[]{:S(2)}) collective-permute-start(bf16[144,768]{1,0:T(8,128)(2,1)} %reshape.130), channel_id=1, source_target_pairs={{0,2},{2,4},{4,6},{6,0},{1,3},{3,5},{5,7},{7,1},{8,10},{10,12},{12... | collective-permute-start | bytes 663560 | tf_op jit(solution)/shard_map/ppermute | solution.py:14
  54.0 21.1 %collective-permute-start.11 = (bf16[576,768]{1,0:T(8,128)(2,1)S(1)}, bf16[576,768]{1,0:T(8,128)(2,1)S(1)}, u32[]{:S(2)}, u32[]{:S(2)}) collective-permute-start(bf16[576,768]{1,0:T(8,128)(2,1)S(1)} %constant_dynamic-update-slice_fusion.4.refs_0_.y0r), channel_id=1, source_target_pairs={{0,6},{2,0},{4,2},{6,4},{1,7},{3,1},{5,3},{7,5},{8,14},{10,8},{12,... | collective-permute-start | bytes 2654216 | tf_op jit(solution)/shard_map/ppermute | solution.py:14
  56.6 21.6 %collective-permute-start.12 = (bf16[576,768]{1,0:T(8,128)(2,1)S(1)}, bf16[576,768]{1,0:T(8,128)(2,1)S(1)}, u32[]{:S(2)}, u32[]{:S(2)}) collective-permute-start(bf16[576,768]{1,0:T(8,128)(2,1)S(1)} %constant_dynamic-update-slice_fusion.4.refs_0_.y0r), channel_id=1, source_target_pairs={{0,2},{2,4},{4,6},{6,0},{1,3},{3,5},{5,7},{7,1},{8,10},{10,12},{12... | collective-permute-start | bytes 2654216 | tf_op jit(solution)/shard_map/ppermute | solution.py:14
  56.6 3.2 %copy-start.3 = (bf16[3072,1024]{1,0:T(8,128)(2,1)S(1)}, bf16[3072,1024]{1,0:T(8,128)(2,1)}, u32[]{:S(2)}) copy-start(bf16[3072,1024]{1,0:T(8,128)(2,1)} %copy-done.2) | copy-start | bytes 18874372
  56.7 21.5 %collective-permute-start.6 = (bf16[144,3072]{1,0:T(8,128)(2,1)S(1)}, bf16[144,3072]{1,0:T(8,128)(2,1)S(1)}, u32[]{:S(2)}, u32[]{:S(2)}) collective-permute-start(bf16[144,3072]{1,0:T(8,128)(2,1)S(1)} %constant_dynamic-update-slice_fusion.refs_0_.xrr), channel_id=1, source_target_pairs={{0,192},{64,0},{128,64},{192,128},{1,193},{65,1},{129,65},{193,129... | collective-permute-start | bytes 2654216 | tf_op jit(solution)/shard_map/ppermute | solution.py:14
  59.1 19.8 %collective-permute-start.7 = (bf16[144,3072]{1,0:T(8,128)(2,1)S(1)}, bf16[144,3072]{1,0:T(8,128)(2,1)S(1)}, u32[]{:S(2)}, u32[]{:S(2)}) collective-permute-start(bf16[144,3072]{1,0:T(8,128)(2,1)S(1)} %constant_dynamic-update-slice_fusion.refs_0_.xrr), channel_id=1, source_target_pairs={{0,64},{64,128},{128,192},{192,0},{1,65},{65,129},{129,193},{193,1... | collective-permute-start | bytes 2654216 | tf_op jit(solution)/shard_map/ppermute | solution.py:14
  79.0 8.5 %collective-permute-start.13 = (bf16[144,1536]{1,0:T(8,128)(2,1)S(1)}, bf16[144,1536]{1,0:T(8,128)(2,1)S(1)}, u32[]{:S(2)}, u32[]{:S(2)}) collective-permute-start(bf16[144,1536]{1,0:T(8,128)(2,1)S(1)} %slice.106), channel_id=1, source_target_pairs={{0,192},{64,0},{128,64},{192,128},{1,193},{65,1},{129,65},{193,129... | collective-permute-start | bytes 1327112 | tf_op jit(solution)/shard_map/ppermute | solution.py:14
  79.5 9.5 %collective-permute-start.14 = (bf16[144,1536]{1,0:T(8,128)(2,1)S(1)}, bf16[144,1536]{1,0:T(8,128)(2,1)S(1)}, u32[]{:S(2)}, u32[]{:S(2)}) collective-permute-start(bf16[144,1536]{1,0:T(8,128)(2,1)S(1)} %slice.107), channel_id=1, source_target_pairs={{0,64},{64,128},{128,192},{192,0},{1,65},{65,129},{129,193},{193,1... | collective-permute-start | bytes 1327112 | tf_op jit(solution)/shard_map/ppermute | solution.py:14
  80.8 8.2 %collective-permute-start.15 = (bf16[288,768]{1,0:T(8,128)(2,1)S(1)}, bf16[288,768]{1,0:T(8,128)(2,1)S(1)}, u32[]{:S(2)}, u32[]{:S(2)}) collective-permute-start(bf16[288,768]{1,0:T(8,128)(2,1)S(1)} %slice.108), channel_id=1, source_target_pairs={{0,6},{2,0},{4,2},{6,4},{1,7},{3,1},{5,3},{7,5},{8,14},{10,8},{12,... | collective-permute-start | bytes 1327112 | tf_op jit(solution)/shard_map/ppermute | solution.py:14
  81.9 8.7 %collective-permute-start.16 = (bf16[288,768]{1,0:T(8,128)(2,1)S(1)}, bf16[288,768]{1,0:T(8,128)(2,1)S(1)}, u32[]{:S(2)}, u32[]{:S(2)}) collective-permute-start(bf16[288,768]{1,0:T(8,128)(2,1)S(1)} %slice.109), channel_id=1, source_target_pairs={{0,2},{2,4},{4,6},{6,0},{1,3},{3,5},{5,7},{7,1},{8,10},{10,12},{12... | collective-permute-start | bytes 1327112 | tf_op jit(solution)/shard_map/ppermute | solution.py:14
  99.0 12.0 %collective-permute-start.17 = (bf16[288,384]{1,0:T(8,128)(2,1)S(1)}, bf16[288,384]{1,0:T(8,128)(2,1)S(1)}, u32[]{:S(2)}, u32[]{:S(2)}) collective-permute-start(bf16[288,384]{1,0:T(8,128)(2,1)S(1)} %get-tuple-element.69), channel_id=1, source_target_pairs={{0,2},{2,4},{4,6},{6,0},{1,3},{3,5},{5,7},{7,1},{8,10},{10,12},{12... | collective-permute-start | bytes 663560 | tf_op jit(solution)/shard_map/ppermute | solution.py:14
  99.1 11.9 %collective-permute-start.18 = (bf16[288,384]{1,0:T(8,128)(2,1)S(1)}, bf16[288,384]{1,0:T(8,128)(2,1)S(1)}, u32[]{:S(2)}, u32[]{:S(2)}) collective-permute-start(bf16[288,384]{1,0:T(8,128)(2,1)S(1)} %get-tuple-element.68), channel_id=1, source_target_pairs={{0,6},{2,0},{4,2},{6,4},{1,7},{3,1},{5,3},{7,5},{8,14},{10,8},{12,... | collective-permute-start | bytes 663560 | tf_op jit(solution)/shard_map/ppermute | solution.py:14
  101.8 9.1 %collective-permute-start.19 = (bf16[144,768]{1,0:T(8,128)(2,1)S(1)}, bf16[144,768]{1,0:T(8,128)(2,1)S(1)}, u32[]{:S(2)}, u32[]{:S(2)}) collective-permute-start(bf16[144,768]{1,0:T(8,128)(2,1)S(1)} %get-tuple-element.63), channel_id=1, source_target_pairs={{0,64},{64,128},{128,192},{192,0},{1,65},{65,129},{129,193},{193,1... | collective-permute-start | bytes 663560 | tf_op jit(solution)/shard_map/ppermute | solution.py:14
  101.9 9.1 %collective-permute-start.20 = (bf16[144,768]{1,0:T(8,128)(2,1)S(1)}, bf16[144,768]{1,0:T(8,128)(2,1)S(1)}, u32[]{:S(2)}, u32[]{:S(2)}) collective-permute-start(bf16[144,768]{1,0:T(8,128)(2,1)S(1)} %get-tuple-element.62), channel_id=1, source_target_pairs={{0,192},{64,0},{128,64},{192,128},{1,193},{65,1},{129,65},{193,129... | collective-permute-start | bytes 663560 | tf_op jit(solution)/shard_map/ppermute | solution.py:14
  110.9 40.3 %collective-permute-start.31 = (bf16[3072,768]{1,0:T(8,128)(2,1)}, bf16[3072,768]{1,0:T(8,128)(2,1)}, u32[]{:S(2)}, u32[]{:S(2)}) collective-permute-start(bf16[3072,768]{1,0:T(8,128)(2,1)} %shard_map.108), channel_id=1, source_target_pairs={{0,1},{1,0},{2,3},{3,2},{4,5},{5,4},{6,7},{7,6},{8,9},{9,8},{10,11... | collective-permute-start | bytes 14155784 | tf_op jit(solution)/shard_map/ppermute | solution.py:18
  117.8 11.9 %collective-permute-start.24 = (bf16[144,1536]{1,0:T(8,128)(2,1)S(1)}, bf16[144,1536]{1,0:T(8,128)(2,1)S(1)}, u32[]{:S(2)}, u32[]{:S(2)}) collective-permute-start(bf16[144,1536]{1,0:T(8,128)(2,1)S(1)} %pad_maximum_fusion.4), channel_id=1, source_target_pairs={{0,192},{64,0},{128,64},{192,128},{1,193},{65,1},{129,65},{193,129... | collective-permute-start | bytes 1327112 | tf_op jit(solution)/shard_map/ppermute | solution.py:14
  118.3 13.0 %collective-permute-start.23 = (bf16[144,1536]{1,0:T(8,128)(2,1)S(1)}, bf16[144,1536]{1,0:T(8,128)(2,1)S(1)}, u32[]{:S(2)}, u32[]{:S(2)}) collective-permute-start(bf16[144,1536]{1,0:T(8,128)(2,1)S(1)} %pad_maximum_fusion.3), channel_id=1, source_target_pairs={{0,64},{64,128},{128,192},{192,0},{1,65},{65,129},{129,193},{193,1... | collective-permute-start | bytes 1327112 | tf_op jit(solution)/shard_map/ppermute | solution.py:14
  119.8 11.4 %collective-permute-start.22 = (bf16[576,384]{1,0:T(8,128)(2,1)S(1)}, bf16[576,384]{1,0:T(8,128)(2,1)S(1)}, u32[]{:S(2)}, u32[]{:S(2)}) collective-permute-start(bf16[576,384]{1,0:T(8,128)(2,1)S(1)} %pad_maximum_fusion.2), channel_id=1, source_target_pairs={{0,6},{2,0},{4,2},{6,4},{1,7},{3,1},{5,3},{7,5},{8,14},{10,8},{12,... | collective-permute-start | bytes 1327112 | tf_op jit(solution)/shard_map/ppermute | solution.py:14
  120.0 12.4 %collective-permute-start.21 = (bf16[576,384]{1,0:T(8,128)(2,1)S(1)}, bf16[576,384]{1,0:T(8,128)(2,1)S(1)}, u32[]{:S(2)}, u32[]{:S(2)}) collective-permute-start(bf16[576,384]{1,0:T(8,128)(2,1)S(1)} %pad_maximum_fusion.1), channel_id=1, source_target_pairs={{0,2},{2,4},{4,6},{6,0},{1,3},{3,5},{5,7},{7,1},{8,10},{10,12},{12... | collective-permute-start | bytes 1327112 | tf_op jit(solution)/shard_map/ppermute | solution.py:14
  126.9 2.2 %copy-start.4 = (bf16[3072,768]{1,0:T(8,128)(2,1)}, bf16[3072,768]{1,0:T(8,128)(2,1)S(1)}, u32[]{:S(2)}) copy-start(bf16[3072,768]{1,0:T(8,128)(2,1)S(1)} %shard_map.109.a) | copy-start | bytes 14155780
  132.7 4.9 %collective-permute-start.25 = (bf16[144,384]{1,0:T(8,128)(2,1)S(1)}, bf16[144,384]{1,0:T(8,128)(2,1)S(1)}, u32[]{:S(2)}, u32[]{:S(2)}) collective-permute-start(bf16[144,384]{1,0:T(8,128)(2,1)S(1)} %get-tuple-element.74), channel_id=1, source_target_pairs={{0,64},{64,128},{128,192},{192,0},{1,65},{65,129},{129,193},{193,1... | collective-permute-start | bytes 331784 | tf_op jit(solution)/shard_map/ppermute | solution.py:14
  133.1 6.2 %collective-permute-start.26 = (bf16[144,384]{1,0:T(8,128)(2,1)S(1)}, bf16[144,384]{1,0:T(8,128)(2,1)S(1)}, u32[]{:S(2)}, u32[]{:S(2)}) collective-permute-start(bf16[144,384]{1,0:T(8,128)(2,1)S(1)} %get-tuple-element.76), channel_id=1, source_target_pairs={{0,128},{64,192},{128,0},{192,64},{1,129},{65,193},{129,1},{193,65... | collective-permute-start | bytes 331784 | tf_op jit(solution)/shard_map/ppermute | solution.py:14
  135.5 4.3 %collective-permute-start.27 = (bf16[144,384]{1,0:T(8,128)(2,1)S(1)}, bf16[144,384]{1,0:T(8,128)(2,1)S(1)}, u32[]{:S(2)}, u32[]{:S(2)}) collective-permute-start(bf16[144,384]{1,0:T(8,128)(2,1)S(1)} %get-tuple-element.75), channel_id=1, source_target_pairs={{0,192},{64,0},{128,64},{192,128},{1,193},{65,1},{129,65},{193,129... | collective-permute-start | bytes 331784 | tf_op jit(solution)/shard_map/ppermute | solution.py:14
  135.8 5.2 %collective-permute-start.28 = (bf16[144,384]{1,0:T(8,128)(2,1)S(1)}, bf16[144,384]{1,0:T(8,128)(2,1)S(1)}, u32[]{:S(2)}, u32[]{:S(2)}) collective-permute-start(bf16[144,384]{1,0:T(8,128)(2,1)S(1)} %get-tuple-element.77), channel_id=1, source_target_pairs={{0,2},{2,4},{4,6},{6,0},{1,3},{3,5},{5,7},{7,1},{8,10},{10,12},{12... | collective-permute-start | bytes 331784 | tf_op jit(solution)/shard_map/ppermute | solution.py:14
  137.5 5.2 %collective-permute-start.29 = (bf16[144,384]{1,0:T(8,128)(2,1)S(1)}, bf16[144,384]{1,0:T(8,128)(2,1)S(1)}, u32[]{:S(2)}, u32[]{:S(2)}) collective-permute-start(bf16[144,384]{1,0:T(8,128)(2,1)S(1)} %get-tuple-element.79), channel_id=1, source_target_pairs={{0,4},{2,6},{4,0},{6,2},{1,5},{3,7},{5,1},{7,3},{8,12},{10,14},{12... | collective-permute-start | bytes 331784 | tf_op jit(solution)/shard_map/ppermute | solution.py:14
  139.3 3.9 %collective-permute-start.30 = (bf16[144,384]{1,0:T(8,128)(2,1)S(1)}, bf16[144,384]{1,0:T(8,128)(2,1)S(1)}, u32[]{:S(2)}, u32[]{:S(2)}) collective-permute-start(bf16[144,384]{1,0:T(8,128)(2,1)S(1)} %get-tuple-element.78), channel_id=1, source_target_pairs={{0,6},{2,0},{4,2},{6,4},{1,7},{3,1},{5,3},{7,5},{8,14},{10,8},{12,... | collective-permute-start | bytes 331784 | tf_op jit(solution)/shard_map/ppermute | solution.py:14
  144.1 19.6 %all-to-all-start.1 = ((bf16[16,18,384]{2,1,0:T(8,128)(2,1)}), bf16[16,18,384]{2,1,0:T(8,128)(2,1)S(1)}, u32[]{:S(2)}, u32[]{:S(2)}) async-start(bf16[16,18,384]{2,1,0:T(8,128)(2,1)} %bitcast.24), calls=%async_computation.1 | async-start | bytes 589824 | tf_op jit(solution)/shard_map/all_to_all | solution.py:401
  151.2 2.3 %copy-start.5 = (bf16[3072,768]{1,0:T(8,128)(2,1)S(1)}, bf16[3072,768]{1,0:T(8,128)(2,1)}, u32[]{:S(2)}) copy-start(bf16[3072,768]{1,0:T(8,128)(2,1)} %copy-done.4) | copy-start | bytes 14155780
  153.6 11.3 %copy-start.1 = (bf16[128,3072]{1,0:T(8,128)(2,1)S(1)}, bf16[128,3072]{1,0:T(8,128)(2,1)}, u32[]{:S(2)}) copy-start(bf16[128,3072]{1,0:T(8,128)(2,1)} %param.8) | copy-start | bytes 2359300
where the time goes:
time: 166 us; the launch traced here: 165 us
  starting transfers between devices  53.6 us (32%)
  waiting for transfers between devices  43.8 us (26%)
  Pallas kernels  35.6 us (21%)
  local copies, waits for them, and re-layouts  26.3 us (16%)
  matrix products  2.49 us (2%)
  other arithmetic  2.05 us (1%)
    pallas_call x9, Pallas kernels, call(): pl.pallas_call(body, grid_spec=pltpu.PrefetchScalarGridSpec(num_scalar_pr...  35.6 us
    ppermute x28, waiting for transfers between devices, turn(): return lax.ppermute(a, axis, [(i, (i + step) % size) for i in range(size)])  34.6 us
    ppermute x28, starting transfers between devices, turn(): return lax.ppermute(a, axis, [(i, (i + step) % size) for i in range(size)])  29.4 us
    unnamed x28, local copies, waits for them, and re-layouts  17.9 us
    ppermute x4, starting transfers between devices, swap(): return lax.ppermute(a, 'core', [(0, 1), (1, 0)])  10.5 us
    all_to_all x1, starting transfers between devices, shards(): lax.all_to_all(back, ('expert', 'core'), split_axis=0, concat_axis=0, til...  7.14 us
    all_to_all x1, starting transfers between devices, shards(): lax.all_to_all(sent, 'expert', split_axis=0, concat_axis=0, tiled=True)  6.47 us
    all_to_all x1, waiting for transfers between devices, shards(): lax.all_to_all(back, ('expert', 'core'), split_axis=0, concat_axis=0, til...  4.78 us
  transfers between devices with their start and end apart: 34, of which 18 were waited for; matrix products, arithmetic and copies ran while one was open for 7% of the time, Pallas kernels for 17%

commit v1 on v0

v1 whole, which is shorter than its diff:
```python
import jax
import jax.numpy as jnp
from jax import lax
from jax.experimental import pallas as pl
from jax.experimental.pallas import tpu as pltpu
from jax.sharding import Mesh, PartitionSpec as P

BF = jnp.bfloat16
F32 = jnp.float32


def turn(a, axis, step):
    size = lax.axis_size(axis)
    return lax.ppermute(a, axis, [(i, (i + step) % size) for i in range(size)])


def swap(a):
    return lax.ppermute(a, "core", [(0, 1), (1, 0)])


def ring(a, second, step, cross=False):
    nd, nx = lax.axis_size("dp"), lax.axis_size("x")
    pairs = []
    for d in range(nd):
        for x in range(nx):
            for c in range(2):
                along_x = (c == 0) != second
                to_d, to_x = (d, (x + step) % nx) if along_x else ((d + step) % nd, x)
                to_c = 1 - c if cross else c
                pairs.append(((d * nx + x) * 2 + c, (to_d * nx + to_x) * 2 + to_c))
    return lax.ppermute(a, ("dp", "x", "core"), pairs)


def dot(a, b, dims):
    return lax.dot_general(a, b, (dims, ((), ())), preferred_element_type=F32)


def same(shape):
    return pl.BlockSpec(shape, lambda k, xi: (0,) * len(shape), pipeline_mode=pl.Buffered(1))


def call(body, grid, in_specs, out_specs, out_shape, args, flops, mib, scratch=()):
    return pl.pallas_call(
        body,
        grid_spec=pltpu.PrefetchScalarGridSpec(
            num_scalar_prefetch=1,
            grid=grid,
            in_specs=in_specs,
            out_specs=out_specs,
            scratch_shapes=scratch,
        ),
        out_shape=out_shape,
        compiler_params=pltpu.CompilerParams(
            dimension_semantics=("arbitrary",), vmem_limit_bytes=mib << 20
        ),
        cost_estimate=pl.CostEstimate(flops=int(flops), bytes_accessed=8 << 20, transcendentals=0),
    )(*args)


def dispatch(xi, ids, gates, tokens, grad_out, slots, cols):
    experts = lax.axis_size("expert")
    every, rows = experts * slots, tokens.shape[0]

    def body(xi, ids, gates, tok, grad, sent, pick):
        j = lax.broadcasted_iota(jnp.int32, (every, 1), 0)
        e = jnp.zeros((every, 1), jnp.int32)
        for m in range(1, experts):
            e += (j >= m * slots).astype(jnp.int32)
        s = j - e * slots
        first, second = ids[0:1, :] == e, ids[1:2, :] == e
        member = jnp.where(first | second, 1.0, 0.0)
        early = lax.broadcasted_iota(jnp.int32, (rows, rows), 0)
        late = lax.broadcasted_iota(jnp.int32, (rows, rows), 1)
        before = jnp.where(early < late, 1.0, 0.0).astype(BF)
        slot = dot(member.astype(BF), before, ((1,), (0,)))
        hit = jnp.where(slot == s.astype(F32), member, 0.0)
        gate = jnp.where(first, gates[0:1, :], 0.0) + jnp.where(second, gates[1:2, :], 0.0)
        gate = jnp.sum(hit * gate, axis=1, keepdims=True)
        hit = hit.astype(BF)
        pick[...] = hit

        @pl.when(xi[1] == 0)
        def _():
            sent[...] = dot(hit, tok[...], ((1,), (0,))).astype(BF)

        @pl.when(xi[1] == 1)
        def _():
            sent[...] = (dot(hit, grad[...], ((1,), (0,))) * gate).astype(BF)

    column = pl.BlockSpec((rows, cols), lambda k, xi: (0, xi[0]))
    return call(
        body,
        (1,),
        [same(ids.shape), same(gates.shape), column, column],
        [same((every, cols)), same((every, rows))],
        [jax.ShapeDtypeStruct((every, cols), BF), jax.ShapeDtypeStruct((every, rows), BF)],
        (xi, ids, gates, tokens, grad_out),
        2 * every * rows * cols,
        56,
    )


def row_map(out_rows, in_rows, groups, out_size, in_size):
    r = lax.broadcasted_iota(jnp.int32, (out_rows, in_rows), 0)
    q = lax.broadcasted_iota(jnp.int32, (out_rows, in_rows), 1)
    gr, gq = jnp.zeros_like(r), jnp.zeros_like(q)
    for m in range(1, groups):
        gr += (r >= m * out_size).astype(jnp.int32)
        gq += (q >= m * in_size).astype(jnp.int32)
    match = (gr == gq) & (r - gr * out_size == q - gq * in_size)
    return jnp.where(match, 1.0, 0.0).astype(BF)


def compact(xi, got, groups, capacity):
    rows, cols = got.shape
    every = groups * capacity

    def body(xi, a, out):
        m = row_map(every, rows, groups, capacity, rows // groups)
        out[...] = dot(m, a[...], ((1,), (0,))).astype(BF)

    return call(
        body,
        (1,),
        [same((rows, cols))],
        same((every, cols)),
        jax.ShapeDtypeStruct((every, cols), BF),
        (xi, got),
        2 * every * rows * cols,
        8,
    )


def spread(xi, parts, groups, slots):
    two, half, cols = parts[0].shape
    rows = groups * slots

    def body(xi, *refs):
        *ins, out = refs
        total = ins[0][...].astype(F32)
        for a in ins[1:]:
            total += a[...].astype(F32)
        total = total.astype(BF)
        low = jnp.where(xi[1] == 0, total[0], total[1])
        high = jnp.where(xi[1] == 0, total[1], total[0])
        m = row_map(rows, 2 * half, groups, slots, 2 * half // groups)
        out[...] = dot(m, jnp.concatenate([low, high], axis=0), ((1,), (0,))).astype(BF)

    return call(
        body,
        (1,),
        [same((two, half, cols))] * len(parts),
        same((rows, cols)),
        jax.ShapeDtypeStruct((rows, cols), BF),
        (xi, *parts),
        4 * rows * half * cols,
        8,
    )


def pack(xi, own, theirs):
    width, hid = own[0].shape
    cols = width // 4
    up = pl.BlockSpec((cols, hid), lambda k, xi: ((xi[0] + k) % 4, 0))
    down = pl.BlockSpec((hid, cols), lambda k, xi: (0, (xi[0] + k) % 4))

    def body(xi, g1, u1, d1, g2, u2, d2, w, wd):
        for j, ref in enumerate((g1, u1, g2, u2)):
            w[:, j * hid : (j + 1) * hid] = ref[...]
        wd[:hid] = d1[...]
        wd[hid:] = d2[...]

    return call(
        body,
        (4,),
        [up, up, down] * 2,
        [
            pl.BlockSpec((cols, 4 * hid), lambda k, xi: (k, 0)),
            pl.BlockSpec((2 * hid, cols), lambda k, xi: (0, k)),
        ],
        [jax.ShapeDtypeStruct((width, 4 * hid), BF), jax.ShapeDtypeStruct((2 * hid, width), BF)],
        (xi, *own, *theirs),
        width * hid,
        14,
    )


def hidden_part(xi, pieces, w):
    _, rows, cols = pieces[0].shape
    width = 4 * cols
    every = rows * len(pieces)

    def body(xi, *refs):
        *xs, w, out = refs
        a = xs[0][0] if len(xs) == 1 else jnp.concatenate([x[0] for x in xs], axis=0)
        part = dot(a, w[...], ((1,), (0,)))
        first = pl.program_id(0) == 0

        @pl.when(first)
        def _():
            out[...] = part

        @pl.when(jnp.logical_not(first))
        def _():
            out[...] += part

    shape = jax.ShapeDtypeStruct((every, w.shape[1]), F32)
    return call(
        body,
        (4,),
        [pl.BlockSpec((1, rows, cols), lambda k, xi: (k, 0, 0))] * len(pieces)
        + [pl.BlockSpec((cols, w.shape[1]), lambda k, xi: (k, 0))],
        same(shape.shape),
        shape,
        (xi, *pieces, w),
        2 * every * width * w.shape[1],
        14,
    )


def down_part(xi, ys, places, wd, so_far=None):
    rows, cols = ys[0].shape
    n = len(ys)
    more = [] if so_far is None else [so_far]

    def body(xi, *refs):
        out = dot(refs[0][...], refs[n][...], ((1,), (1,)))
        for j in range(1, n):
            out += dot(refs[j][...], refs[n + j][...], ((1,), (1,)))
        if more:
            out += refs[2 * n][...]
        refs[-1][...] = out

    shape = jax.ShapeDtypeStruct((rows, wd.shape[0]), F32)
    return call(
        body,
        (1,),
        [same((rows, cols))] * n
        + [pl.BlockSpec((wd.shape[0], cols), lambda k, xi, j=j: (0, j)) for j in places]
        + [same(shape.shape)] * len(more),
        same(shape.shape),
        shape,
        (xi, *ys, *(wd,) * n, *more),
        2 * n * rows * cols * wd.shape[0],
        16,
    )


def token_part(xi, hu0, hu13, ga, x2a, x2b, y2a, y2b, w, wd):
    _, rows, cols = x2a.shape
    width = 4 * cols
    hid = w.shape[1] // 4
    every = 4 * rows

    def body(xi, h0, h13, ga1, xa, xb, ya, yb, w, wd, act, g, keep, send, h2):
        step = pl.program_id(0)

        @pl.when(step < 4)
        def _():
            part = dot(jnp.where(step < 2, xa[0], xb[0]), w[...], ((1,), (0,)))

            @pl.when(step == 0)
            def _():
                h2[...] = part

            @pl.when(step > 0)
            def _():
                h2[...] += part

        @pl.when(step == 3)
        def _():
            y2 = jnp.concatenate([ya[...], yb[...]], axis=0)
            for c in range(2):
                part = slice(c * hid, (c + 1) * hid)
                hs = slice(2 * c * hid, (2 * c + 1) * hid)
                us = slice((2 * c + 1) * hid, (2 * c + 2) * hid)
                ga2 = dot(y2, wd[part, :], ((1,), (1,)))
                for k, (ref, at) in enumerate(((h0, 0), (h13, 0), (h2, 0), (h13, rows))):
                    r = slice(k * rows, (k + 1) * rows)
                    hh = ref[at : at + rows, hs]
                    uu = ref[at : at + rows, us]
                    gg = ga1[r, part] + ga2[r]
                    s = jax.nn.sigmoid(hh)
                    silu = hh * s
                    act[r, part] = (silu * uu).astype(BF)
                    g[r, hs] = (gg * uu * (s * (1.0 + hh * (1.0 - s)))).astype(BF)
                    g[r, us] = (gg * silu).astype(BF)

        @pl.when(step > 3)
        def _():
            out = dot(g[...], w[...], ((1,), (1,))).astype(BF)
            for mine, by_x, by_y in ((0, keep, send), (1, send, keep)):

                @pl.when(xi[1] == mine)
                def _():
                    for j in range(4):
                        r = slice(j * rows, (j + 1) * rows)
                        by_x[step - 4, j] = out[r, : cols // 2]
                        by_y[j, step - 4] = out[r, cols // 2 :]

    shapes = [
        jax.ShapeDtypeStruct((every, 2 * hid), BF),
        jax.ShapeDtypeStruct((every, 4 * hid), BF),
        jax.ShapeDtypeStruct((4, 4, rows, cols // 2), BF),
        jax.ShapeDtypeStruct((4, 4, rows, cols // 2), BF),
    ]
    return call(
        body,
        (8,),
        [same(a.shape) for a in (hu0, hu13, ga)]
        + [
            pl.BlockSpec((1, rows, cols), lambda k, xi: (jnp.minimum(k, 1), 0, 0)),
            pl.BlockSpec((1, rows, cols), lambda k, xi: (jnp.clip(k - 2, 0, 1), 0, 0)),
            same(y2a.shape),
            same(y2b.shape),
            pl.BlockSpec((cols, 4 * hid), lambda k, xi: (k % 4, 0)),
            pl.BlockSpec((2 * hid, cols), lambda k, xi: (0, 2), pipeline_mode=pl.Buffered(1)),
        ],
        [same(a.shape) for a in shapes],
        shapes,
        (xi, hu0, hu13, ga, x2a, x2b, y2a, y2b, w, wd),
        2 * every * width * 4 * hid,
        24,
        [pltpu.VMEM((rows, 4 * hid), F32)],
    )


def weight_part(xi, xs, ys, act, g, which, rest=None):
    xr, x1, x2a, x2b, x3 = xs
    _, rows, cols = xr.shape
    width = 4 * cols
    every = 4 * rows
    hid = act.shape[1] // 2
    x_spec = pl.BlockSpec((1, rows, cols), lambda k, xi: (k, 0, 0))
    a_spec = pl.BlockSpec((1, rows, cols), lambda k, xi: (jnp.minimum(k, 1), 0, 0))
    b_spec = pl.BlockSpec((1, rows, cols), lambda k, xi: (jnp.maximum(k - 2, 0), 0, 0))
    part = pl.BlockSpec((cols, 3 * hid), lambda k, xi: (k, 0))

    def body(xi, xrr, x1r, xar, xbr, x3r, y0r, y1r, yar, ybr, y3r, actr, gr, *refs):
        ybuf = refs[-1]
        k = pl.program_id(0)
        for j, y in ((0, y0r), (1, y1r), (3, y3r)):

            @pl.when(k == j)
            def _():
                ybuf[...] = y[...]

        @pl.when(k == 2)
        def _():
            ybuf[: every // 2] = yar[...]
            ybuf[every // 2 :] = ybr[...]

        x2 = jnp.where(k < 2, xar[0], xbr[0])
        x = jnp.concatenate([xrr[0], x1r[0], x2, x3r[0]], axis=0)
        up = dot(x, gr[...], ((0,), (0,)))
        d = dot(actr[...], ybuf[...], ((0,), (0,)))
        squares = [slice(j * hid, (j + 1) * hid) for j in range(cols // hid)]
        if rest is None:
            refs[0][:, : 2 * hid] = up.astype(BF)
            for c in squares:
                refs[0][c, 2 * hid :] = d[:, c].astype(BF)
        else:
            other, og, ou, od = refs[:4]
            og[...] = (up[:, :hid] + other[:, :hid].astype(F32)).astype(BF)
            ou[...] = (up[:, hid:] + other[:, hid : 2 * hid].astype(F32)).astype(BF)
            for c in squares:
                od[:, c] = (d[:, c] + other[c, 2 * hid :].astype(F32)).astype(BF)

    up = pl.BlockSpec((cols, hid), lambda k, xi: ((xi[0] + k) % 4, 0))
    down = pl.BlockSpec((hid, cols), lambda k, xi: (0, (xi[0] + k) % 4))
    return call(
        body,
        (4,),
        [x_spec, x_spec, a_spec, b_spec, x_spec]
        + [same(y.shape) for y in ys]
        + [
            pl.BlockSpec((every, hid), lambda k, xi: (0, which), pipeline_mode=pl.Buffered(1)),
            pl.BlockSpec((every, 2 * hid), lambda k, xi: (0, which), pipeline_mode=pl.Buffered(1)),
        ]
        + ([] if rest is None else [part]),
        part if rest is None else [up, up, down],
        jax.ShapeDtypeStruct((width, 3 * hid), BF)
        if rest is None
        else [
            jax.ShapeDtypeStruct((width, hid), BF),
            jax.ShapeDtypeStruct((width, hid), BF),
            jax.ShapeDtypeStruct((hid, width), BF),
        ],
        (xi, *xs, *ys, act, g) + (() if rest is None else (rest,)),
        2 * 3 * every * width * hid,
        22,
        [pltpu.VMEM((every, cols), BF)],
    )


def add(*parts):
    out = parts[0].astype(F32)
    for p in parts[1:]:
        out = out + p.astype(F32)
    return out.astype(BF)


def tie(values, *late):
    out = lax.optimization_barrier((tuple(values), tuple(late)))
    return out[0]


def shards(tokens, grad_out, gate_prob, expert_ids, w_gate, w_up, w_down):
    rows, width = tokens.shape
    experts = lax.axis_size("expert")
    nx = lax.axis_size("x")
    capacity = rows * 9 // (4 * experts)
    cols = width // nx
    slots = (capacity + 7) // 8 * 8
    half = experts * capacity // 2
    xi = lax.axis_index("x")
    core = lax.axis_index("core")
    on0 = core == 0
    at = jnp.stack([xi, core]).astype(jnp.int32)
    own = (w_gate[0], w_up[0], w_down[0])
    theirs = [swap(w) for w in own]

    sent, pick = dispatch(at, expert_ids.T, gate_prob.T, tokens, grad_out, slots, cols)
    sent = sent.reshape(experts, slots, cols)
    got = lax.all_to_all(sent, "expert", split_axis=0, concat_axis=0, tiled=True)
    got, on0 = tie((got, on0), *theirs)
    got = compact(at, got.reshape(experts * slots, cols), experts, capacity)
    w, wd = pack(at, own, theirs)

    p0 = jnp.stack([got, ring(got, False, -1), ring(got, False, 2), ring(got, False, 1)])

    def sort(kept, come):
        return jnp.where(on0, kept, come), jnp.where(on0, come, kept)

    def flat(y):
        return y.reshape(-1, cols)

    stay = jnp.where(on0, p0[:, :half], p0[:, half:])
    leave = jnp.where(on0, p0[:, half:], p0[:, :half])
    s1, c1 = ring(stay, True, -1), ring(leave, True, -1, cross=True)
    s3, c3 = ring(stay, True, 1), ring(leave, True, 1, cross=True)
    x0, y0 = sort(stay, swap(leave))
    hu0 = hidden_part(at, (x0,), w)
    ga0 = down_part(at, (flat(y0),), (0,), wd)
    s1, c1, s3, c3 = tie((s1, c1, s3, c3), hu0, ga0)
    x1, y1 = sort(s1, c1)
    x3, y3 = sort(s3, c3)
    x2a, x2b = turn(x1[:2], "dp", -1), turn(x3[2:], "dp", 1)
    y2a, y2b = turn(y1[:2], "x", -1), turn(y3[2:], "x", 1)
    hu13 = hidden_part(at, (x1, x3), w)
    ga = down_part(at, (flat(y1), flat(y3)), (1, 3), wd, ga0)
    x2a, x2b, y2a, y2b = tie((x2a, x2b, y2a, y2b), hu13, ga)
    y_all = [flat(y) for y in (y0, y1, y2a, y2b, y3)]
    x_all = (x0, x1, x2a, x2b, x3)
    act, g, keep, send = token_part(at, hu0, hu13, ga, x2a, x2b, y_all[2], y_all[3], w, wd)

    k_up, k_dn = ring(keep[2], False, 1), ring(keep[3], False, -1)
    come = swap(send)
    v_dn, v_up = ring(come[2], False, -1), ring(come[1], False, 1)
    part = weight_part(at, x_all, y_all, act, g, 1)
    k_up, k_dn, v_up, v_dn, part = tie((k_up, k_dn, v_up, v_dn, part))
    k_up = ring(add(keep[1], k_up), False, 1)
    v_dn = ring(add(come[3], v_dn), False, -1)
    part = swap(part)
    total = jnp.stack([add(keep[0], k_up, k_dn), add(come[0], v_up, v_dn)], axis=1)
    parts = [ring(total[k], True, k) for k in (1, 2, 3)]
    gw_gate, gw_up, gw_down = weight_part(at, x_all, y_all, act, g, 0, part)
    parts = tie(parts, gw_gate)
    back = spread(at, [total[0], *parts], experts, slots)

    back = back.reshape(experts, slots, cols // 2)
    back = lax.all_to_all(back, "expert", split_axis=0, concat_axis=0, tiled=True)
    back = back.reshape(experts * slots, cols // 2)
    grad_tokens = dot(pick, back, ((0,), (0,))).astype(BF)
    return grad_tokens, gw_gate[None], gw_up[None], gw_down[None]


def solution(mesh):
    sizes = mesh.devices.shape
    fine = Mesh(
        mesh.devices.reshape(sizes[0], sizes[1], sizes[2] // 2, 2), ("dp", "expert", "x", "core")
    )
    by_token = P(("dp", "expert"), None)
    up = P("expert", None, ("dp", "x", "core"))
    down = P("expert", ("dp", "x", "core"), None)
    return jax.shard_map(
        shards,
        mesh=fine,
        in_specs=(by_token, by_token, by_token, by_token, up, up, down),
        out_specs=(P(("dp", "expert"), ("x", "core")), up, up, down),
        check_vma=False,
    )
```

time: 166 us -> 150 us (0.904)
  local copies, waits for them, and re-layouts: 26.3 us -> 0.33 us
  starting transfers between devices: 53.6 us -> 41.2 us
  blocking collectives: 0 us -> 11.4 us
  waiting for transfers between devices: 43.8 us -> 52.9 us
  Pallas kernels: 35.6 us -> 38.6 us
    ppermute x28 -> x4, waiting for transfers between devices: 34.6 us -> 2.9 us  [turn(): return lax.ppermute(a, axis, [(i, (i + step) % size) for i in range(size)])]
    ppermute x0 -> x16, waiting for transfers between devices: none -> 31 us  [ring(): return lax.ppermute(a, ('dp', 'x', 'core'), pairs)]
    ppermute x28 -> x4, starting transfers between devices: 29.4 us -> 5.87 us  [turn(): return lax.ppermute(a, axis, [(i, (i + step) % size) for i in range(size)])]
    ppermute x0 -> x16, starting transfers between devices: none -> 18.1 us  [ring(): return lax.ppermute(a, ('dp', 'x', 'core'), pairs)]
    unnamed x28 -> x10, local copies, waits for them, and re-layouts: 17.9 us -> 0.03 us
    all_to_all x1, waiting for transfers between devices: 4.42 us -> 17.3 us  [shards(): lax.all_to_all(sent, 'expert', split_axis=0, concat_axis=0, tiled=True)]
    all_to_all x0 -> x1, blocking collectives: none -> 11.4 us  [shards(): lax.all_to_all(back, 'expert', split_axis=0, concat_axis=0, tiled=True)]
    all_to_all x1 -> x0, starting transfers between devices: 7.14 us -> none  [shards(): lax.all_to_all(back, ('expert', 'core'), split_axis=0, concat_axis=0, til...]
  transfers between devices with their start and end apart: 34 -> 27, of which waited for: 18 -> 12; matrix products, arithmetic and copies ran while one was open for 7% -> 1% of each run, Pallas kernels for 17% -> 19%
where the time goes in v1:
time: 150 us; the launch traced here: 148 us
  waiting for transfers between devices  52.9 us (35%)
  starting transfers between devices  41.2 us (27%)
  Pallas kernels  38.6 us (26%)
  blocking collectives  11.4 us (8%)
  other arithmetic  2.05 us (1%)
    pallas_call x11, Pallas kernels, call(): pl.pallas_call(body, grid_spec=pltpu.PrefetchScalarGridSpec(num_scalar_pr...  38.6 us
    ppermute x16, waiting for transfers between devices, ring(): return lax.ppermute(a, ('dp', 'x', 'core'), pairs)  31 us
    ppermute x16, starting transfers between devices, ring(): return lax.ppermute(a, ('dp', 'x', 'core'), pairs)  18.1 us
    all_to_all x1, waiting for transfers between devices, shards(): lax.all_to_all(sent, 'expert', split_axis=0, concat_axis=0, tiled=True)  17.3 us
    all_to_all x1, blocking collectives, shards(): lax.all_to_all(back, 'expert', split_axis=0, concat_axis=0, tiled=True)  11.4 us
    ppermute x6, starting transfers between devices, swap(): return lax.ppermute(a, 'core', [(0, 1), (1, 0)])  10.7 us
    all_to_all x1, starting transfers between devices, shards(): lax.all_to_all(sent, 'expert', split_axis=0, concat_axis=0, tiled=True)  6.47 us
    ppermute x4, starting transfers between devices, turn(): return lax.ppermute(a, axis, [(i, (i + step) % size) for i in range(size)])  5.87 us
  transfers between devices with their start and end apart: 27, of which 12 were waited for; matrix products, arithmetic and copies ran while one was open for 1% of the time, Pallas kernels for 19%

profile of v1, /device:TPU:1, one launch (start us, length us, event | category | flops | bytes accessed | tf_op | source)
XLA Modules:
  0.0 148.3 jit_solution(5797158960694039026)
XLA Ops:
  0.6 3.3 %collective-permute-start = (bf16[3072,256]{1,0:T(8,128)(2,1)}, bf16[3072,256]{1,0:T(8,128)(2,1)S(1)}, u32[]{:S(2)}, u32[]{:S(2)}) collective-permute-start(bf16[3072,256]{1,0:T(8,128)(2,1)} %bitcast.78), channel_id=1, source_target_pairs={{0,1},{1,0},{2,3},{3,2},{4,5},{5,4},{6,7},{7,6},{8,9},{9,8},{10,11... | collective-permute-start | bytes 4718600 | tf_op jit(solution)/shard_map/ppermute | solution.py:18
  4.1 0.4 collective-permute-start.2
  4.5 0.6 pad_add_fusion.xi
  5.1 3.2 %shard_map.102 = (bf16[320,768]{1,0:T(8,128)(2,1)}, bf16[320,128]{1,0:T(8,128)(2,1)}) custom-call(s32[2]{0:T(128)} %pad_add_fusion.xi, s32[2,128]{1,0:T(2,128)} %bitcast.90, f32[2,128]{1,0:T(2,128)} %bitcast.91, bf16[128,3072]{1,0:T(8,128)(2,1)} %tok.1, bf16[128,3072]{1,0:T(8,128)(2,1)} %grad.1), custom_call_target="tpu_custom_call" | custom-call | flops 62914560 | bytes 8388608 | tf_op jit(solution)/shard_map/pallas_call | solution.py:43
  8.2 6.5 %all-to-all-start = ((bf16[8,40,768]{2,1,0:T(8,128)(2,1)}), bf16[8,40,768]{2,1,0:T(8,128)(2,1)S(1)}, u32[]{:S(2)}, u32[]{:S(2)}) async-start(bf16[8,40,768]{2,1,0:T(8,128)(2,1)} %bitcast.86), calls=%async_computation | async-start | bytes 983040 | tf_op jit(solution)/shard_map/all_to_all | solution.py:425
  14.7 17.3 %all-to-all-done = bf16[8,40,768]{2,1,0:T(8,128)(2,1)S(1)} async-done(((bf16[8,40,768]{2,1,0:T(8,128)(2,1)}), bf16[8,40,768]{2,1,0:T(8,128)(2,1)S(1)}, u32[]{:S(2)}, u32[]{:S(2)}) %all-to-all-start) | async-done | bytes 491552 | tf_op jit(solution)/shard_map/all_to_all | solution.py:425
  32.0 0.9 shard_map.103
  32.9 1.4 collective-permute-start.5
  34.3 2.6 %collective-permute-start.4 = (bf16[288,768]{1,0:T(8,128)(2,1)S(1)}, bf16[288,768]{1,0:T(8,128)(2,1)S(1)}, u32[]{:S(2)}, u32[]{:S(2)}) collective-permute-start(bf16[288,768]{1,0:T(8,128)(2,1)S(1)} %shard_map.103), channel_id=1, source_target_pairs={{0,4},{1,129},{2,6},{3,131},{4,0},{5,133},{6,2},{7,135},{64,68},{6... | collective-permute-start | bytes 1327112 | tf_op jit(solution)/shard_map/ppermute | solution.py:31
  36.9 1.1 collective-permute-start.3
  38.0 3.7 %collective-permute-done.5 = bf16[288,768]{1,0:T(8,128)(2,1)S(1)} collective-permute-done((bf16[288,768]{1,0:T(8,128)(2,1)S(1)}, bf16[288,768]{1,0:T(8,128)(2,1)S(1)}, u32[]{:S(2)}, u32[]{:S(2)}) %collective-permute-start.5) | collective-permute-done | bytes 442400 | tf_op jit(solution)/shard_map/ppermute | solution.py:31
  41.7 5.9 %collective-permute-done.4 = bf16[288,768]{1,0:T(8,128)(2,1)S(1)} collective-permute-done((bf16[288,768]{1,0:T(8,128)(2,1)S(1)}, bf16[288,768]{1,0:T(8,128)(2,1)S(1)}, u32[]{:S(2)}, u32[]{:S(2)}) %collective-permute-start.4) | collective-permute-done | bytes 442400 | tf_op jit(solution)/shard_map/ppermute | solution.py:31
  48.0 1.2 collective-permute-start.6
  49.2 1.6 %collective-permute-start.10 = (bf16[4,144,768]{2,1,0:T(8,128)(2,1)S(1)}, bf16[4,144,768]{2,1,0:T(8,128)(2,1)S(1)}, u32[]{:S(2)}, u32[]{:S(2)}) collective-permute-start(bf16[4,144,768]{2,1,0:T(8,128)(2,1)S(1)} %broadcast_select_fusion.6), channel_id=1, source_target_pairs={{0,65},{1,2},{2,67},{3,4},{4,69},{5,6},{6,71},{7,0},{64,129},{65,6... | collective-permute-start | bytes 2654216 | tf_op jit(solution)/shard_map/ppermute | solution.py:31
  50.8 2.2 %collective-permute-start.8 = (bf16[4,144,768]{2,1,0:T(8,128)(2,1)S(1)}, bf16[4,144,768]{2,1,0:T(8,128)(2,1)S(1)}, u32[]{:S(2)}, u32[]{:S(2)}) collective-permute-start(bf16[4,144,768]{2,1,0:T(8,128)(2,1)S(1)} %broadcast_select_fusion.6), channel_id=1, source_target_pairs={{0,193},{1,6},{2,195},{3,0},{4,197},{5,2},{6,199},{7,4},{64,1},{65... | collective-permute-start | bytes 2654216 | tf_op jit(solution)/shard_map/ppermute | solution.py:31
  53.2 2.7 %collective-permute-start.7 = (bf16[4,144,768]{2,1,0:T(8,128)(2,1)S(1)}, bf16[4,144,768]{2,1,0:T(8,128)(2,1)S(1)}, u32[]{:S(2)}, u32[]{:S(2)}) collective-permute-start(bf16[4,144,768]{2,1,0:T(8,128)(2,1)S(1)} %get-tuple-element.63), channel_id=1, source_target_pairs={{0,192},{1,7},{2,194},{3,1},{4,196},{5,3},{6,198},{7,5},{64,0},{65... | collective-permute-start | bytes 2654216 | tf_op jit(solution)/shard_map/ppermute | solution.py:31
  55.9 4.0 %shard_map.104 = (bf16[3072,1024]{1,0:T(8,128)(2,1)S(1)}, bf16[512,3072]{1,0:T(8,128)(2,1)S(1)}) custom-call(s32[2]{0:T(128)S(1)} %copy-done.3, bf16[3072,256]{1,0:T(8,128)(2,1)S(1)} %bitcast.79, bf16[3072,256]{1,0:T(8,128)(2,1)S(1)} %bitcast.81, bf16[256,3072]{1,0:T(8,128)(2,1)S(1)} %bitcast.83, bf16[3072,256]{1,0:T(8,128)(2,1)S(1)} %collective-permute-done.g2, ...), custom_call_target="tpu_custom_call" | custom-call | flops 786432 | bytes 8388608 | tf_op jit(solution)/shard_map/pallas_call | solution.py:43
  60.0 1.2 shard_map.106.refs_4_
  61.3 2.4 %shard_map.105.h0 = f32[144,1024]{1,0:T(8,128)S(1)} custom-call(s32[2]{0:T(128)S(1)} %copy-done.3, bf16[4,144,768]{2,1,0:T(8,128)(2,1)S(1)} %broadcast_select_fusion.5.refs_0_.xrr, bf16[3072,1024]{1,0:T(8,128)(2,1)S(1)} %get-tuple-element.37.refs_1_.refs_2_.w), custom_call_target="tpu_custom_call" | custom-call | flops 905969664 | bytes 8388608 | tf_op jit(solution)/shard_map/pallas_call | solution.py:43
  63.7 8.3 %collective-permute-done.9 = bf16[4,144,768]{2,1,0:T(8,128)(2,1)S(1)} collective-permute-done((bf16[4,144,768]{2,1,0:T(8,128)(2,1)S(1)}, bf16[4,144,768]{2,1,0:T(8,128)(2,1)S(1)}, u32[]{:S(2)}, u32[]{:S(2)}) %collective-permute-start.9) | collective-permute-done | bytes 884768 | tf_op jit(solution)/shard_map/ppermute | solution.py:31
  72.0 0.5 collective-permute-done.7
  72.9 1.4 collective-permute-start.12
  74.3 1.4 collective-permute-start.14
  75.6 1.5 %collective-permute-start.11 = (bf16[2,144,768]{2,1,0:T(8,128)(2,1)S(1)}, bf16[2,144,768]{2,1,0:T(8,128)(2,1)S(1)}, u32[]{:S(2)}, u32[]{:S(2)}) collective-permute-start(bf16[2,144,768]{2,1,0:T(8,128)(2,1)S(1)} %slice.76), channel_id=1, source_target_pairs={{0,192},{64,0},{128,64},{192,128},{1,193},{65,1},{129,65},{193,129... | collective-permute-start | bytes 1327112 | tf_op jit(solution)/shard_map/ppermute | solution.py:14
  77.2 1.6 %collective-permute-start.13 = (bf16[2,144,768]{2,1,0:T(8,128)(2,1)S(1)}, bf16[2,144,768]{2,1,0:T(8,128)(2,1)S(1)}, u32[]{:S(2)}, u32[]{:S(2)}) collective-permute-start(bf16[2,144,768]{2,1,0:T(8,128)(2,1)S(1)} %slice.78), channel_id=1, source_target_pairs={{0,6},{2,0},{4,2},{6,4},{1,7},{3,1},{5,3},{7,5},{8,14},{10,8},{12,... | collective-permute-start | bytes 1327112 | tf_op jit(solution)/shard_map/ppermute | solution.py:14
  78.8 1.6 %shard_map.108.ga1 = f32[576,512]{1,0:T(8,128)S(1)} custom-call(s32[2]{0:T(128)S(1)} %copy-done.3, bf16[576,768]{1,0:T(8,128)(2,1)S(1)} %bitcast.61, bf16[576,768]{1,0:T(8,128)(2,1)S(1)} %bitcast.64, bf16[512,3072]{1,0:T(8,128)(2,1)S(1)} %get-tuple-element.38.refs_1_.refs_2_.refs_3_.wd, bf16[512,3072]{1,0:T(8,128)(2,1)S(1)} %get-tuple-element.38.refs_1_.refs_2_.refs_3_.wd, ...), custom_call_target="tpu_custom_call" | custom-call | flops 905969664 | bytes 8388608 | tf_op jit(solution)/shard_map/pallas_call | solution.py:43
  80.4 3.5 %shard_map.107.h13 = f32[288,1024]{1,0:T(8,128)S(1)} custom-call(s32[2]{0:T(128)S(1)} %copy-done.3, bf16[4,144,768]{2,1,0:T(8,128)(2,1)S(1)} %get-tuple-element.71.refs_0_.x1r, bf16[4,144,768]{2,1,0:T(8,128)(2,1)S(1)} %get-tuple-element.69.refs_1_.x3r, bf16[3072,1024]{1,0:T(8,128)(2,1)S(1)} %get-tuple-element.37.refs_1_.refs_2_.w), custom_call_target="tpu_custom_call" | custom-call | flops 1811939328 | bytes 8388608 | tf_op jit(solution)/shard_map/pallas_call | solution.py:43
  84.0 2.9 %collective-permute-done.14 = bf16[2,144,768]{2,1,0:T(8,128)(2,1)S(1)} collective-permute-done((bf16[2,144,768]{2,1,0:T(8,128)(2,1)S(1)}, bf16[2,144,768]{2,1,0:T(8,128)(2,1)S(1)}, u32[]{:S(2)}, u32[]{:S(2)}) %collective-permute-start.14) | collective-permute-done | bytes 442400 | tf_op jit(solution)/shard_map/ppermute | solution.py:14
  86.9 8.6 %shard_map.109 = (bf16[576,512]{1,0:T(8,128)(2,1)S(1)}, bf16[576,1024]{1,0:T(8,128)(2,1)S(1)}, bf16[4,4,144,384]{3,2,1,0:T(8,128)(2,1)S(1)}, bf16[4,4,144,384]{3,2,1,0:T(8,128)(2,1)S(1)}) custom-call(s32[2]{0:T(128)S(1)} %copy-done.3, f32[144,1024]{1,0:T(8,128)S(1)} %shard_map.105.h0, f32[288,1024]{1,0:T(8,128)S(1)} %shard_map.107.h13, ...), custom_call_target="tpu_custom_call" | custom-call | flops 3623878656 | bytes 8388608 | tf_op jit(solution)/shard_map/pallas_call | solution.py:43
  95.5 3.0 %collective-permute-start.17 = (bf16[4,4,144,384]{3,2,1,0:T(8,128)(2,1)S(1)}, bf16[4,4,144,384]{3,2,1,0:T(8,128)(2,1)S(1)}, u32[]{:S(2)}, u32[]{:S(2)}) collective-permute-start(bf16[4,4,144,384]{3,2,1,0:T(8,128)(2,1)S(1)} %get-tuple-element.48), channel_id=1, source_target_pairs={{0,1},{1,0},{2,3},{3,2},{4,5},{5,4},{6,7},{7,6},{8,9},{9,8},{10,11... | collective-permute-start | bytes 5308424 | tf_op jit(solution)/shard_map/ppermute | solution.py:18
  98.6 1.3 collective-permute-start.16
  99.9 0.2 collective-permute-start.15
  100.1 1.7 %collective-permute-done.17 = bf16[4,4,144,384]{3,2,1,0:T(8,128)(2,1)S(1)} collective-permute-done((bf16[4,4,144,384]{3,2,1,0:T(8,128)(2,1)S(1)}, bf16[4,4,144,384]{3,2,1,0:T(8,128)(2,1)S(1)}, u32[]{:S(2)}, u32[]{:S(2)}) %collective-permute-start.17) | collective-permute-done | bytes 1769504 | tf_op jit(solution)/shard_map/ppermute | solution.py:18
  101.9 1.3 collective-permute-start.19
  103.5 5.5 %shard_map.110 = bf16[3072,768]{1,0:T(8,128)(2,1)S(1)} custom-call(s32[2]{0:T(128)S(1)} %copy-done.3, bf16[4,144,768]{2,1,0:T(8,128)(2,1)S(1)} %broadcast_select_fusion.5.refs_0_.xrr, bf16[4,144,768]{2,1,0:T(8,128)(2,1)S(1)} %get-tuple-element.71.refs_0_.x1r, bf16[2,144,768]{2,1,0:T(8,128)(2,1)S(1)} %collective-permute-done.11.xa.xar, ...), custom_call_target="tpu_custom_call" | custom-call | flops 2717908992 | bytes 8388608 | tf_op jit(solution)/shard_map/pallas_call | solution.py:43
  109.0 1.8 %collective-permute-done.19 = bf16[4,144,384]{2,1,0:T(8,128)(2,1)S(1)} collective-permute-done((bf16[4,144,384]{2,1,0:T(8,128)(2,1)S(1)}, bf16[4,144,384]{2,1,0:T(8,128)(2,1)S(1)}, u32[]{:S(2)}, u32[]{:S(2)}) %collective-permute-start.19) | collective-permute-done | bytes 442400 | tf_op jit(solution)/shard_map/ppermute | solution.py:31
  110.9 2.4 %collective-permute-done.18 = bf16[4,144,384]{2,1,0:T(8,128)(2,1)S(1)} collective-permute-done((bf16[4,144,384]{2,1,0:T(8,128)(2,1)S(1)}, bf16[4,144,384]{2,1,0:T(8,128)(2,1)S(1)}, u32[]{:S(2)}, u32[]{:S(2)}) %collective-permute-start.18) | collective-permute-done | bytes 442400 | tf_op jit(solution)/shard_map/ppermute | solution.py:31
  113.3 2.7 %collective-permute-start.25 = (bf16[3072,768]{1,0:T(8,128)(2,1)S(1)}, bf16[3072,768]{1,0:T(8,128)(2,1)S(1)}, u32[]{:S(2)}, u32[]{:S(2)}) collective-permute-start(bf16[3072,768]{1,0:T(8,128)(2,1)S(1)} %shard_map.110), channel_id=1, source_target_pairs={{0,1},{1,0},{2,3},{3,2},{4,5},{5,4},{6,7},{7,6},{8,9},{9,8},{10,11... | collective-permute-start | bytes 14155784 | tf_op jit(solution)/shard_map/ppermute | solution.py:18
  116.1 0.7 collective-permute-start.21
  117.0 1.1 collective-permute-start.20
  118.1 5.6 %collective-permute-done.21 = bf16[4,144,384]{2,1,0:T(8,128)(2,1)S(1)} collective-permute-done((bf16[4,144,384]{2,1,0:T(8,128)(2,1)S(1)}, bf16[4,144,384]{2,1,0:T(8,128)(2,1)S(1)}, u32[]{:S(2)}, u32[]{:S(2)}) %collective-permute-start.21) | collective-permute-done | bytes 442400 | tf_op jit(solution)/shard_map/ppermute | solution.py:31
  123.8 2.0 %collective-permute-done.20 = bf16[4,144,384]{2,1,0:T(8,128)(2,1)S(1)} collective-permute-done((bf16[4,144,384]{2,1,0:T(8,128)(2,1)S(1)}, bf16[4,144,384]{2,1,0:T(8,128)(2,1)S(1)}, u32[]{:S(2)}, u32[]{:S(2)}) %collective-permute-start.20) | collective-permute-done | bytes 442400 | tf_op jit(solution)/shard_map/ppermute | solution.py:31
  126.2 1.5 collective-permute-start.22
  127.7 6.6 %shard_map.111 = (bf16[3072,256]{1,0:T(8,128)(2,1)}, bf16[3072,256]{1,0:T(8,128)(2,1)}, bf16[256,3072]{1,0:T(8,128)(2,1)}) custom-call(s32[2]{0:T(128)S(1)} %copy-done.3, bf16[4,144,768]{2,1,0:T(8,128)(2,1)S(1)} %broadcast_select_fusion.5.refs_0_.xrr, bf16[4,144,768]{2,1,0:T(8,128)(2,1)S(1)} %get-tuple-element.71.refs_0_.x1r, ...), custom_call_target="tpu_custom_call" | custom-call | flops 2717908992 | bytes 8388608 | tf_op jit(solution)/shard_map/pallas_call | solution.py:43
  134.3 0.7 collective-permute-done.22.refs_1_
  135.0 0.9 shard_map.112
  135.9 11.4 %all_to_all.10 = bf16[8,40,384]{2,1,0:T(8,128)(2,1)S(1)} all-to-all(bf16[8,40,384]{2,1,0:T(8,128)(2,1)S(1)} %bitcast.84), channel_id=1, replica_groups=mesh['dp'=4,'expert'=8,'x'=4,'core'=2] {'expert'}, dimensions={0} | all-to-all | bytes 491520 | tf_op jit(solution)/shard_map/all_to_all | solution.py:472
  147.4 0.9 convolution_convert_fusion
  (47 shorter events, 2.3 us)
Async XLA Ops:
  0.6 31.3 %collective-permute-start = (bf16[3072,256]{1,0:T(8,128)(2,1)}, bf16[3072,256]{1,0:T(8,128)(2,1)S(1)}, u32[]{:S(2)}, u32[]{:S(2)}) collective-permute-start(bf16[3072,256]{1,0:T(8,128)(2,1)} %bitcast.78), channel_id=1, source_target_pairs={{0,1},{1,0},{2,3},{3,2},{4,5},{5,4},{6,7},{7,6},{8,9},{9,8},{10,11... | collective-permute-start | bytes 4718600 | tf_op jit(solution)/shard_map/ppermute | solution.py:18
  4.0 28.0 %collective-permute-start.1 = (bf16[3072,256]{1,0:T(8,128)(2,1)}, bf16[3072,256]{1,0:T(8,128)(2,1)}, u32[]{:S(2)}, u32[]{:S(2)}) collective-permute-start(bf16[3072,256]{1,0:T(8,128)(2,1)} %bitcast.80), channel_id=1, source_target_pairs={{0,1},{1,0},{2,3},{3,2},{4,5},{5,4},{6,7},{7,6},{8,9},{9,8},{10,11... | collective-permute-start | bytes 4718600 | tf_op jit(solution)/shard_map/ppermute | solution.py:18
  4.1 27.9 %collective-permute-start.2 = (bf16[256,3072]{1,0:T(8,128)(2,1)}, bf16[256,3072]{1,0:T(8,128)(2,1)}, u32[]{:S(2)}, u32[]{:S(2)}) collective-permute-start(bf16[256,3072]{1,0:T(8,128)(2,1)} %bitcast.82), channel_id=1, source_target_pairs={{0,1},{1,0},{2,3},{3,2},{4,5},{5,4},{6,7},{7,6},{8,9},{9,8},{10,11... | collective-permute-start | bytes 4718600 | tf_op jit(solution)/shard_map/ppermute | solution.py:18
  5.1 26.9 %copy-start.3 = (s32[2]{0:T(128)S(1)}, s32[2]{0:T(128)}, u32[]{:S(2)}) copy-start(s32[2]{0:T(128)} %pad_add_fusion.xi) | copy-start | bytes 28
  8.2 23.7 %all-to-all-start = ((bf16[8,40,768]{2,1,0:T(8,128)(2,1)}), bf16[8,40,768]{2,1,0:T(8,128)(2,1)S(1)}, u32[]{:S(2)}, u32[]{:S(2)}) async-start(bf16[8,40,768]{2,1,0:T(8,128)(2,1)} %bitcast.86), calls=%async_computation | async-start | bytes 983040 | tf_op jit(solution)/shard_map/all_to_all | solution.py:425
  32.9 8.8 %collective-permute-start.5 = (bf16[288,768]{1,0:T(8,128)(2,1)S(1)}, bf16[288,768]{1,0:T(8,128)(2,1)S(1)}, u32[]{:S(2)}, u32[]{:S(2)}) collective-permute-start(bf16[288,768]{1,0:T(8,128)(2,1)S(1)} %shard_map.103), channel_id=1, source_target_pairs={{0,2},{1,65},{2,4},{3,67},{4,6},{5,69},{6,0},{7,71},{64,66},{65,12... | collective-permute-start | bytes 1327112 | tf_op jit(solution)/shard_map/ppermute | solution.py:31
  34.3 13.3 %collective-permute-start.4 = (bf16[288,768]{1,0:T(8,128)(2,1)S(1)}, bf16[288,768]{1,0:T(8,128)(2,1)S(1)}, u32[]{:S(2)}, u32[]{:S(2)}) collective-permute-start(bf16[288,768]{1,0:T(8,128)(2,1)S(1)} %shard_map.103), channel_id=1, source_target_pairs={{0,4},{1,129},{2,6},{3,131},{4,0},{5,133},{6,2},{7,135},{64,68},{6... | collective-permute-start | bytes 1327112 | tf_op jit(solution)/shard_map/ppermute | solution.py:31
  36.9 10.7 %collective-permute-start.3 = (bf16[288,768]{1,0:T(8,128)(2,1)S(1)}, bf16[288,768]{1,0:T(8,128)(2,1)S(1)}, u32[]{:S(2)}, u32[]{:S(2)}) collective-permute-start(bf16[288,768]{1,0:T(8,128)(2,1)S(1)} %shard_map.103), channel_id=1, source_target_pairs={{0,6},{1,193},{2,0},{3,195},{4,2},{5,197},{6,4},{7,199},{64,70},{6... | collective-permute-start | bytes 1327112 | tf_op jit(solution)/shard_map/ppermute | solution.py:31
  47.9 8.0 %copy-start.2 = (bf16[1,256,3072]{2,1,0:T(8,128)(2,1)S(1)}, bf16[1,256,3072]{2,1,0:T(8,128)(2,1)}, u32[]{:S(2)}) copy-start(bf16[1,256,3072]{2,1,0:T(8,128)(2,1)} %param.13) | copy-start | bytes 4718596
  48.0 7.9 %copy-start = (bf16[1,3072,256]{2,1,0:T(8,128)(2,1)S(1)}, bf16[1,3072,256]{2,1,0:T(8,128)(2,1)}, u32[]{:S(2)}) copy-start(bf16[1,3072,256]{2,1,0:T(8,128)(2,1)} %param.11) | copy-start | bytes 4718596
  48.0 7.9 %copy-start.1 = (bf16[1,3072,256]{2,1,0:T(8,128)(2,1)S(1)}, bf16[1,3072,256]{2,1,0:T(8,128)(2,1)}, u32[]{:S(2)}) copy-start(bf16[1,3072,256]{2,1,0:T(8,128)(2,1)} %param.12) | copy-start | bytes 4718596
  48.0 5.0 %collective-permute-start.6 = (bf16[4,144,768]{2,1,0:T(8,128)(2,1)S(1)}, bf16[4,144,768]{2,1,0:T(8,128)(2,1)S(1)}, u32[]{:S(2)}, u32[]{:S(2)}) collective-permute-start(bf16[4,144,768]{2,1,0:T(8,128)(2,1)S(1)} %broadcast_select_fusion.6), channel_id=1, source_target_pairs={{0,1},{1,0},{2,3},{3,2},{4,5},{5,4},{6,7},{7,6},{8,9},{9,8},{10,11... | collective-permute-start | bytes 2654216 | tf_op jit(solution)/shard_map/ppermute | solution.py:18
  49.2 14.5 %collective-permute-start.10 = (bf16[4,144,768]{2,1,0:T(8,128)(2,1)S(1)}, bf16[4,144,768]{2,1,0:T(8,128)(2,1)S(1)}, u32[]{:S(2)}, u32[]{:S(2)}) collective-permute-start(bf16[4,144,768]{2,1,0:T(8,128)(2,1)S(1)} %broadcast_select_fusion.6), channel_id=1, source_target_pairs={{0,65},{1,2},{2,67},{3,4},{4,69},{5,6},{6,71},{7,0},{64,129},{65,6... | collective-permute-start | bytes 2654216 | tf_op jit(solution)/shard_map/ppermute | solution.py:31
  50.8 13.0 %collective-permute-start.8 = (bf16[4,144,768]{2,1,0:T(8,128)(2,1)S(1)}, bf16[4,144,768]{2,1,0:T(8,128)(2,1)S(1)}, u32[]{:S(2)}, u32[]{:S(2)}) collective-permute-start(bf16[4,144,768]{2,1,0:T(8,128)(2,1)S(1)} %broadcast_select_fusion.6), channel_id=1, source_target_pairs={{0,193},{1,6},{2,195},{3,0},{4,197},{5,2},{6,199},{7,4},{64,1},{65... | collective-permute-start | bytes 2654216 | tf_op jit(solution)/shard_map/ppermute | solution.py:31
  53.2 18.9 %collective-permute-start.9 = (bf16[4,144,768]{2,1,0:T(8,128)(2,1)S(1)}, bf16[4,144,768]{2,1,0:T(8,128)(2,1)S(1)}, u32[]{:S(2)}, u32[]{:S(2)}) collective-permute-start(bf16[4,144,768]{2,1,0:T(8,128)(2,1)S(1)} %get-tuple-element.63), channel_id=1, source_target_pairs={{0,64},{1,3},{2,66},{3,5},{4,68},{5,7},{6,70},{7,1},{64,128},{65,6... | collective-permute-start | bytes 2654216 | tf_op jit(solution)/shard_map/ppermute | solution.py:31
  53.2 19.2 %collective-permute-start.7 = (bf16[4,144,768]{2,1,0:T(8,128)(2,1)S(1)}, bf16[4,144,768]{2,1,0:T(8,128)(2,1)S(1)}, u32[]{:S(2)}, u32[]{:S(2)}) collective-permute-start(bf16[4,144,768]{2,1,0:T(8,128)(2,1)S(1)} %get-tuple-element.63), channel_id=1, source_target_pairs={{0,192},{1,7},{2,194},{3,1},{4,196},{5,3},{6,198},{7,5},{64,0},{65... | collective-permute-start | bytes 2654216 | tf_op jit(solution)/shard_map/ppermute | solution.py:31
  72.9 11.1 %collective-permute-start.12 = (bf16[2,144,768]{2,1,0:T(8,128)(2,1)S(1)}, bf16[2,144,768]{2,1,0:T(8,128)(2,1)S(1)}, u32[]{:S(2)}, u32[]{:S(2)}) collective-permute-start(bf16[2,144,768]{2,1,0:T(8,128)(2,1)S(1)} %slice.77), channel_id=1, source_target_pairs={{0,64},{64,128},{128,192},{192,0},{1,65},{65,129},{129,193},{193,1... | collective-permute-start | bytes 1327112 | tf_op jit(solution)/shard_map/ppermute | solution.py:14
  74.3 12.6 %collective-permute-start.14 = (bf16[2,144,768]{2,1,0:T(8,128)(2,1)S(1)}, bf16[2,144,768]{2,1,0:T(8,128)(2,1)S(1)}, u32[]{:S(2)}, u32[]{:S(2)}) collective-permute-start(bf16[2,144,768]{2,1,0:T(8,128)(2,1)S(1)} %slice.79), channel_id=1, source_target_pairs={{0,2},{2,4},{4,6},{6,0},{1,3},{3,5},{5,7},{7,1},{8,10},{10,12},{12... | collective-permute-start | bytes 1327112 | tf_op jit(solution)/shard_map/ppermute | solution.py:14
  75.6 11.2 %collective-permute-start.11 = (bf16[2,144,768]{2,1,0:T(8,128)(2,1)S(1)}, bf16[2,144,768]{2,1,0:T(8,128)(2,1)S(1)}, u32[]{:S(2)}, u32[]{:S(2)}) collective-permute-start(bf16[2,144,768]{2,1,0:T(8,128)(2,1)S(1)} %slice.76), channel_id=1, source_target_pairs={{0,192},{64,0},{128,64},{192,128},{1,193},{65,1},{129,65},{193,129... | collective-permute-start | bytes 1327112 | tf_op jit(solution)/shard_map/ppermute | solution.py:14
  77.2 9.7 %collective-permute-start.13 = (bf16[2,144,768]{2,1,0:T(8,128)(2,1)S(1)}, bf16[2,144,768]{2,1,0:T(8,128)(2,1)S(1)}, u32[]{:S(2)}, u32[]{:S(2)}) collective-permute-start(bf16[2,144,768]{2,1,0:T(8,128)(2,1)S(1)} %slice.78), channel_id=1, source_target_pairs={{0,6},{2,0},{4,2},{6,4},{1,7},{3,1},{5,3},{7,5},{8,14},{10,8},{12,... | collective-permute-start | bytes 1327112 | tf_op jit(solution)/shard_map/ppermute | solution.py:14
  95.5 6.3 %collective-permute-start.17 = (bf16[4,4,144,384]{3,2,1,0:T(8,128)(2,1)S(1)}, bf16[4,4,144,384]{3,2,1,0:T(8,128)(2,1)S(1)}, u32[]{:S(2)}, u32[]{:S(2)}) collective-permute-start(bf16[4,4,144,384]{3,2,1,0:T(8,128)(2,1)S(1)} %get-tuple-element.48), channel_id=1, source_target_pairs={{0,1},{1,0},{2,3},{3,2},{4,5},{5,4},{6,7},{7,6},{8,9},{9,8},{10,11... | collective-permute-start | bytes 5308424 | tf_op jit(solution)/shard_map/ppermute | solution.py:18
  98.6 10.4 %collective-permute-start.16 = (bf16[4,144,384]{2,1,0:T(8,128)(2,1)S(1)}, bf16[4,144,384]{2,1,0:T(8,128)(2,1)S(1)}, u32[]{:S(2)}, u32[]{:S(2)}) collective-permute-start(bf16[4,144,384]{2,1,0:T(8,128)(2,1)S(1)} %get-tuple-element.66), channel_id=1, source_target_pairs={{0,6},{1,193},{2,0},{3,195},{4,2},{5,197},{6,4},{7,199},{64,70},{6... | collective-permute-start | bytes 1327112 | tf_op jit(solution)/shard_map/ppermute | solution.py:31
  99.9 9.1 %collective-permute-start.15 = (bf16[4,144,384]{2,1,0:T(8,128)(2,1)S(1)}, bf16[4,144,384]{2,1,0:T(8,128)(2,1)S(1)}, u32[]{:S(2)}, u32[]{:S(2)}) collective-permute-start(bf16[4,144,384]{2,1,0:T(8,128)(2,1)S(1)} %get-tuple-element.67), channel_id=1, source_target_pairs={{0,2},{1,65},{2,4},{3,67},{4,6},{5,69},{6,0},{7,71},{64,66},{65,12... | collective-permute-start | bytes 1327112 | tf_op jit(solution)/shard_map/ppermute | solution.py:31
  101.9 8.9 %collective-permute-start.19 = (bf16[4,144,384]{2,1,0:T(8,128)(2,1)S(1)}, bf16[4,144,384]{2,1,0:T(8,128)(2,1)S(1)}, u32[]{:S(2)}, u32[]{:S(2)}) collective-permute-start(bf16[4,144,384]{2,1,0:T(8,128)(2,1)S(1)} %get-tuple-element.64), channel_id=1, source_target_pairs={{0,6},{1,193},{2,0},{3,195},{4,2},{5,197},{6,4},{7,199},{64,70},{6... | collective-permute-start | bytes 1327112 | tf_op jit(solution)/shard_map/ppermute | solution.py:31
  103.2 10.1 %collective-permute-start.18 = (bf16[4,144,384]{2,1,0:T(8,128)(2,1)S(1)}, bf16[4,144,384]{2,1,0:T(8,128)(2,1)S(1)}, u32[]{:S(2)}, u32[]{:S(2)}) collective-permute-start(bf16[4,144,384]{2,1,0:T(8,128)(2,1)S(1)} %get-tuple-element.65), channel_id=1, source_target_pairs={{0,2},{1,65},{2,4},{3,67},{4,6},{5,69},{6,0},{7,71},{64,66},{65,12... | collective-permute-start | bytes 1327112 | tf_op jit(solution)/shard_map/ppermute | solution.py:31
  113.3 14.4 %collective-permute-start.25 = (bf16[3072,768]{1,0:T(8,128)(2,1)S(1)}, bf16[3072,768]{1,0:T(8,128)(2,1)S(1)}, u32[]{:S(2)}, u32[]{:S(2)}) collective-permute-start(bf16[3072,768]{1,0:T(8,128)(2,1)S(1)} %shard_map.110), channel_id=1, source_target_pairs={{0,1},{1,0},{2,3},{3,2},{4,5},{5,4},{6,7},{7,6},{8,9},{9,8},{10,11... | collective-permute-start | bytes 14155784 | tf_op jit(solution)/shard_map/ppermute | solution.py:18
  116.1 7.5 %collective-permute-start.21 = (bf16[4,144,384]{2,1,0:T(8,128)(2,1)S(1)}, bf16[4,144,384]{2,1,0:T(8,128)(2,1)S(1)}, u32[]{:S(2)}, u32[]{:S(2)}) collective-permute-start(bf16[4,144,384]{2,1,0:T(8,128)(2,1)S(1)} %fusion), channel_id=1, source_target_pairs={{0,6},{1,193},{2,0},{3,195},{4,2},{5,197},{6,4},{7,199},{64,70},{6... | collective-permute-start | bytes 1327112 | tf_op jit(solution)/shard_map/ppermute | solution.py:31
  117.0 8.9 %collective-permute-start.20 = (bf16[4,144,384]{2,1,0:T(8,128)(2,1)S(1)}, bf16[4,144,384]{2,1,0:T(8,128)(2,1)S(1)}, u32[]{:S(2)}, u32[]{:S(2)}) collective-permute-start(bf16[4,144,384]{2,1,0:T(8,128)(2,1)S(1)} %fusion.3), channel_id=1, source_target_pairs={{0,2},{1,65},{2,4},{3,67},{4,6},{5,69},{6,0},{7,71},{64,66},{65,12... | collective-permute-start | bytes 1327112 | tf_op jit(solution)/shard_map/ppermute | solution.py:31
  126.2 8.1 %collective-permute-start.24 = (bf16[2,144,384]{2,1,0:T(8,128)(2,1)S(1)}, bf16[2,144,384]{2,1,0:T(8,128)(2,1)S(1)}, u32[]{:S(2)}, u32[]{:S(2)}) collective-permute-start(bf16[2,144,384]{2,1,0:T(8,128)(2,1)S(1)} %get-tuple-element.72), channel_id=1, source_target_pairs={{0,192},{1,7},{2,194},{3,1},{4,196},{5,3},{6,198},{7,5},{64,0},{65... | collective-permute-start | bytes 663560 | tf_op jit(solution)/shard_map/ppermute | solution.py:31
  126.2 8.7 %collective-permute-start.22 = (bf16[2,144,384]{2,1,0:T(8,128)(2,1)S(1)}, bf16[2,144,384]{2,1,0:T(8,128)(2,1)S(1)}, u32[]{:S(2)}, u32[]{:S(2)}) collective-permute-start(bf16[2,144,384]{2,1,0:T(8,128)(2,1)S(1)} %get-tuple-element.74), channel_id=1, source_target_pairs={{0,64},{1,3},{2,66},{3,5},{4,68},{5,7},{6,70},{7,1},{64,128},{65,6... | collective-permute-start | bytes 663560 | tf_op jit(solution)/shard_map/ppermute | solution.py:31
  127.7 19.7 %copy-start.4 = (bf16[320,128]{1,0:T(8,128)(2,1)S(1)}, bf16[320,128]{1,0:T(8,128)(2,1)}, u32[]{:S(2)}) copy-start(bf16[320,128]{1,0:T(8,128)(2,1)} %get-tuple-element.33) | copy-start | bytes 245764
  127.7 7.3 %collective-permute-start.23 = (bf16[2,144,384]{2,1,0:T(8,128)(2,1)S(1)}, bf16[2,144,384]{2,1,0:T(8,128)(2,1)S(1)}, u32[]{:S(2)}, u32[]{:S(2)}) collective-permute-start(bf16[2,144,384]{2,1,0:T(8,128)(2,1)S(1)} %get-tuple-element.75), channel_id=1, source_target_pairs={{0,128},{1,5},{2,130},{3,7},{4,132},{5,1},{6,134},{7,3},{64,192},{... | collective-permute-start | bytes 663560 | tf_op jit(solution)/shard_map/ppermute | solution.py:31
